TPU v7x, 512 devices: a whole 4x8x8 slice. The times are simulated.
512 devices in a mesh: gx: 32 (over z, x_lo, core), gy: 16 (over x_hi, y).
Axes of the slice: x: 4 (x_hi: 2, x_lo: 2; x = x_hi * 2 + x_lo), y: 8, z: 8, core: 2. Of those that a mesh axis runs over, the one named last changes fastest.
Arguments:
- feat_in: bfloat16 [64, 192, 32, 128], P('gx', 'gy'), may hold values from -6 to 6
- conv_out: bfloat16 [64, 192, 32, 128], P('gx', 'gy'), may hold values from -30 to 30
- activ: bfloat16 [64, 192, 32, 128], P('gx', 'gy'), may hold values from -6 to 6
- weight: bfloat16 [3456, 128], replicated, may hold values from -0.109375 to 0.109375
- gain: float32 [128], replicated, may hold values from 0.1 to 1.9
- head: float32 [3, 128], replicated, may hold values from -3 to 3
- labels: int32 [64, 192, 32], P('gx', 'gy'), may hold values from 0 to 2
- grad_up: bfloat16 [64, 192, 32, 128], P('gx', 'gy'), may hold values from -8 to 8
Outputs:
- grad_in: bfloat16 [64, 192, 32, 128], P('gx', 'gy')
- grad_weight: bfloat16 [3456, 128], replicated
- gain_gradient: float32 [128], replicated
- shift_gradient: float32 [128], replicated
All inputs are finite; a program needn't handle non-finite values.
Results may differ from a plain program's by a relative error of at most 0.02.
Values may be sent and summed in bfloat16 or wider, within the bound.
A program may use at most 64 MiB of HBM per device.

v0:
```python
import jax
import jax.numpy as jnp
from jax import lax
from jax.sharding import PartitionSpec as P


def padded_2(shard, sides, width):
    for axis, dim in sides:
        devices, length = (lax.axis_size(axis), shard.shape[dim])
        up = [(i, (i + 1) % devices) for i in range(devices - 1)]
        down = [(j, i) for i, j in up]
        last = lax.slice_in_dim(shard, length - width, length, axis=dim)
        first = lax.slice_in_dim(shard, 0, width, axis=dim)
        before = lax.ppermute(last, axis, up)
        after = lax.ppermute(first, axis, down)
        shard = jnp.concatenate([before, shard, after], axis=dim)
    return shard


def tap_block(padded, sign, step_a, width_x, width_y, width_z):
    pieces = []
    for step_b in (-1, 0, 1):
        for step_c in (-1, 0, 1):
            start_x = 1 + sign * step_a
            start_y = 1 + sign * step_b
            start_z = 1 + sign * step_c
            pieces.append(
                padded[
                    start_x : start_x + width_x,
                    start_y : start_y + width_y,
                    start_z : start_z + width_z,
                ]
            )
    joined = jnp.stack(pieces, axis=3)
    return joined.reshape(width_x * width_y * width_z, 9, padded.shape[3])


def on_device(feat_in, conv_out, activ, weight, gain, head, labels, grad_up):
    width_x, width_y, width_z, chans = feat_in.shape
    voxels = width_x * width_y * width_z
    voxel_total = voxels * lax.axis_size("gx") * lax.axis_size("gy") * 1.0
    hidden_complete = conv_out.astype(jnp.float32)
    first, second = lax.psum(
        (
            jnp.sum(hidden_complete, axis=(0, 1, 2)),
            jnp.sum(hidden_complete * hidden_complete, axis=(0, 1, 2)),
        ),
        ("gx", "gy"),
    )
    channel_mean = first / voxel_total
    inverse_deviation = lax.rsqrt(second / voxel_total - channel_mean * channel_mean + 1e-05)
    normalized_input = (hidden_complete - channel_mean) * inverse_deviation
    act = activ.astype(jnp.float32)
    logits = jnp.einsum("xyzc,kc->xyzk", act, head, precision=lax.Precision.HIGHEST)
    onehot = (labels[..., None] == jnp.arange(head.shape[0], dtype=jnp.int32)).astype(jnp.float32)
    dz = 0.5 * (jax.nn.sigmoid(logits) - onehot)
    ga = grad_up.astype(jnp.float32) + jnp.einsum(
        "xyzk,kc->xyzc", dz, head, precision=lax.Precision.HIGHEST
    )
    normed_gradient = jnp.where(act > 0, ga, 0.01 * ga)
    shift_gradient, gain_gradient = lax.psum(
        (
            jnp.sum(normed_gradient, axis=(0, 1, 2)),
            jnp.sum(normed_gradient * normalized_input, axis=(0, 1, 2)),
        ),
        ("gx", "gy"),
    )
    hidden_gradient = (
        gain
        * inverse_deviation
        * (
            normed_gradient
            - shift_gradient / voxel_total
            - normalized_input * gain_gradient / voxel_total
        )
    ).astype(jnp.bfloat16)
    dpad = padded_2(hidden_gradient, (("gx", 0), ("gy", 1)), 1)
    dpad = jnp.pad(dpad, ((0, 0), (0, 0), (1, 1), (0, 0)))
    xpad = padded_2(feat_in, (("gx", 0), ("gy", 1)), 1)
    xpad = jnp.pad(xpad, ((0, 0), (0, 0), (1, 1), (0, 0)))
    total = jnp.zeros((voxels, chans), jnp.float32)
    blocks = []
    flat_grad = hidden_gradient.reshape(voxels, chans)
    for group in range(3):
        step_a = group - 1
        wgroup = weight[group * 9 * chans : (group + 1) * 9 * chans].reshape(9, chans, chans)
        moved = tap_block(dpad, -1, step_a, width_x, width_y, width_z)
        total = total + jnp.einsum("vko,kio->vi", moved, wgroup, preferred_element_type=jnp.float32)
        shifted = tap_block(xpad, 1, step_a, width_x, width_y, width_z)
        blocks.append(
            jnp.einsum("vki,vo->kio", shifted, flat_grad, preferred_element_type=jnp.float32)
        )
    grad_in = total.reshape(width_x, width_y, width_z, chans).astype(jnp.bfloat16)
    local_weight = jnp.concatenate(blocks, axis=0).reshape(27 * chans, chans)
    grad_weight = lax.psum(local_weight, ("gx", "gy")).astype(jnp.bfloat16)
    return (grad_in, grad_weight, gain_gradient, shift_gradient)


def solution(mesh):
    return jax.shard_map(
        on_device,
        mesh=mesh,
        in_specs=(
            P("gx", "gy", None, None),
            P("gx", "gy", None, None),
            P("gx", "gy", None, None),
            P(),
            P(),
            P(),
            P("gx", "gy", None),
            P("gx", "gy", None, None),
        ),
        out_specs=(P("gx", "gy", None, None), P(), P(), P()),
        check_vma=False,
    )
```

profile of v0, /device:TPU:1, one launch (start us, length us, event | category | flops | bytes accessed | tf_op | source)
XLA Modules:
  0.0 351.0 jit_solution(13893033480290182395)
XLA Ops:
  0.7 1.0 fusion.73
  1.7 4.5 %collective-permute-start.4 = (bf16[1,12,32,128]{3,2,1,0:T(8,128)(2,1)S(1)}, bf16[1,12,32,128]{3,2,1,0:T(8,128)(2,1)S(1)}, u32[]{:S(2)}, u32[]{:S(2)}) collective-permute-start(bf16[1,12,32,128]{3,2,1,0:T(8,128)(2,1)S(1)} %get-tuple-element.71), channel_id=1, source_target_pairs={{0,16},{16,32},{32,48},{48,64},{64,80},{80,96},{96,112},{112,128},... | collective-permute-start | bytes 294920 | tf_op jit(solution)/shard_map/ppermute | solution.py:14
  6.2 5.6 %collective-permute-start.5 = (bf16[1,12,32,128]{3,2,1,0:T(8,128)(2,1)S(1)}, bf16[1,12,32,128]{3,2,1,0:T(8,128)(2,1)S(1)}, u32[]{:S(2)}, u32[]{:S(2)}) collective-permute-start(bf16[1,12,32,128]{3,2,1,0:T(8,128)(2,1)S(1)} %get-tuple-element.70), channel_id=1, source_target_pairs={{16,0},{32,16},{48,32},{64,48},{80,64},{96,80},{112,96},{128,112},... | collective-permute-start | bytes 294920 | tf_op jit(solution)/shard_map/ppermute | solution.py:15
  11.8 1.0 convert_reduce_fusion
  12.9 0.7 copy.12
  13.6 100.5 %all-reduce.3 = (f32[128]{0:T(128)S(1)}, f32[128]{0:T(128)S(1)}) all-reduce(f32[128]{0:T(128)S(1)} %get-tuple-element.7, f32[128]{0:T(128)S(1)} %get-tuple-element.6), channel_id=1, replica_groups=mesh['gx'=32,'gy'=16] {'gx','gy'}, use_global_device_ids=true, to_apply=%region_1.0 | all-reduce | flops 256 | bytes 2048 | tf_op jit(solution)/shard_map/psum | solution.py:43
  114.1 0.7 fusion.67
  114.8 1.8 fusion.8
  116.6 2.0 fusion.66
  118.6 94.6 %all-reduce.2 = (f32[128]{0:T(128)S(1)}, f32[128]{0:T(128)S(1)}) all-reduce(f32[128]{0:T(128)S(1)} %get-tuple-element.5, f32[128]{0:T(128)S(1)} %get-tuple-element.4), channel_id=1, replica_groups=mesh['gx'=32,'gy'=16] {'gx','gy'}, use_global_device_ids=true, to_apply=%region_7.8 | all-reduce | flops 256 | bytes 2048 | tf_op jit(solution)/shard_map/psum | solution.py:61
  213.4 4.0 %collective-permute-start = (bf16[1,12,32,128]{3,2,1,0:T(8,128)(2,1)S(1)}, bf16[1,12,32,128]{3,2,1,0:T(8,128)(2,1)S(1)}, u32[]{:S(2)}, u32[]{:S(2)}) collective-permute-start(bf16[1,12,32,128]{3,2,1,0:T(8,128)(2,1)S(1)} %get-tuple-element.74), channel_id=1, source_target_pairs={{0,16},{16,32},{32,48},{48,64},{64,80},{80,96},{96,112},{112,128},... | collective-permute-start | bytes 294920 | tf_op jit(solution)/shard_map/ppermute | solution.py:14
  217.4 1.9 collective-permute-start.1
  219.6 2.5 collective-permute-start.6
  222.0 1.3 collective-permute-start.7
  224.0 4.6 %collective-permute-start.2 = (bf16[4,1,32,128]{3,2,1,0:T(8,128)(2,1)}, bf16[4,1,32,128]{3,2,1,0:T(8,128)(2,1)}, u32[]{:S(2)}, u32[]{:S(2)}) collective-permute-start(bf16[4,1,32,128]{3,2,1,0:T(8,128)(2,1)} %get-tuple-element.66), channel_id=1, source_target_pairs={{0,1},{1,2},{2,3},{3,4},{4,5},{5,6},{6,7},{7,8},{8,9},{9,10},{10,1... | collective-permute-start | bytes 98312 | tf_op jit(solution)/shard_map/ppermute | solution.py:14
  228.5 1.3 collective-permute-start.3
  231.3 0.7 convolution_bitcast_fusion
  232.0 0.7 convolution_bitcast_fusion.1
  232.7 0.7 convolution_bitcast_fusion.2
  233.6 111.3 %all-reduce.5 = bf16[3456,128]{1,0:T(8,128)(2,1)} all-reduce(f32[3456,128]{1,0:T(8,128)S(1)} %bitcast.202), channel_id=1, replica_groups=mesh['gx'=32,'gy'=16] {'gx','gy'}, use_global_device_ids=true, to_apply=%region_8.9 | all-reduce | flops 442368 | bytes 2654208 | tf_op jit(solution)/shard_map/psum | solution.py:95
  344.9 1.0 select_maximum_fusion.2
  346.6 0.9 maximum_maximum_fusion
  349.1 0.6 convolution_bitcast_fusion.3
  349.7 1.3 fusion.2
  (75 shorter events, 4.5 us)
Async XLA Ops:
  0.6 114.1 %copy-start = (f32[3,128]{1,0:T(4,128)S(1)}, f32[3,128]{1,0:T(4,128)}, u32[]{:S(2)}) copy-start(f32[3,128]{1,0:T(4,128)} %param.13) | copy-start | bytes 4612
  0.6 212.6 %copy-start.3 = (bf16[2,12,32,128]{3,2,1,0:T(8,128)(2,1)S(1)}, bf16[2,12,32,128]{3,2,1,0:T(8,128)(2,1)}, u32[]{:S(2)}) copy-start(bf16[2,12,32,128]{3,2,1,0:T(8,128)(2,1)} %param.9) | copy-start | bytes 589828
  0.7 218.7 %copy-start.2 = (bf16[3456,128]{1,0:T(8,128)(2,1)S(1)}, bf16[3456,128]{1,0:T(8,128)(2,1)}, u32[]{:S(2)}) copy-start(bf16[3456,128]{1,0:T(8,128)(2,1)} %param.11) | copy-start | bytes 2654212
  1.7 217.7 %collective-permute-start.4 = (bf16[1,12,32,128]{3,2,1,0:T(8,128)(2,1)S(1)}, bf16[1,12,32,128]{3,2,1,0:T(8,128)(2,1)S(1)}, u32[]{:S(2)}, u32[]{:S(2)}) collective-permute-start(bf16[1,12,32,128]{3,2,1,0:T(8,128)(2,1)S(1)} %get-tuple-element.71), channel_id=1, source_target_pairs={{0,16},{16,32},{32,48},{48,64},{64,80},{80,96},{96,112},{112,128},... | collective-permute-start | bytes 294920 | tf_op jit(solution)/shard_map/ppermute | solution.py:14
  6.2 213.3 %collective-permute-start.5 = (bf16[1,12,32,128]{3,2,1,0:T(8,128)(2,1)S(1)}, bf16[1,12,32,128]{3,2,1,0:T(8,128)(2,1)S(1)}, u32[]{:S(2)}, u32[]{:S(2)}) collective-permute-start(bf16[1,12,32,128]{3,2,1,0:T(8,128)(2,1)S(1)} %get-tuple-element.70), channel_id=1, source_target_pairs={{16,0},{32,16},{48,32},{64,48},{80,64},{96,80},{112,96},{128,112},... | collective-permute-start | bytes 294920 | tf_op jit(solution)/shard_map/ppermute | solution.py:15
  118.6 100.9 %copy-start.1 = (bf16[2,12,32,128]{3,2,1,0:T(8,128)(2,1)S(1)}, bf16[2,12,32,128]{3,2,1,0:T(8,128)(2,1)}, u32[]{:S(2)}) copy-start(bf16[2,12,32,128]{3,2,1,0:T(8,128)(2,1)} %param.8) | copy-start | bytes 589828
  213.2 6.3 %copy-start.4 = (f32[128]{0:T(128)}, f32[128]{0:T(128)S(1)}, u32[]{:S(2)}) copy-start(f32[128]{0:T(128)S(1)} %get-tuple-element.8) | copy-start | bytes 1540
  213.2 6.3 %copy-start.5 = (f32[128]{0:T(128)}, f32[128]{0:T(128)S(1)}, u32[]{:S(2)}) copy-start(f32[128]{0:T(128)S(1)} %get-tuple-element.9) | copy-start | bytes 1540
  213.4 9.9 %collective-permute-start = (bf16[1,12,32,128]{3,2,1,0:T(8,128)(2,1)S(1)}, bf16[1,12,32,128]{3,2,1,0:T(8,128)(2,1)S(1)}, u32[]{:S(2)}, u32[]{:S(2)}) collective-permute-start(bf16[1,12,32,128]{3,2,1,0:T(8,128)(2,1)S(1)} %get-tuple-element.74), channel_id=1, source_target_pairs={{0,16},{16,32},{32,48},{48,64},{64,80},{80,96},{96,112},{112,128},... | collective-permute-start | bytes 294920 | tf_op jit(solution)/shard_map/ppermute | solution.py:14
  217.4 5.9 %collective-permute-start.1 = (bf16[1,12,32,128]{3,2,1,0:T(8,128)(2,1)S(1)}, bf16[1,12,32,128]{3,2,1,0:T(8,128)(2,1)S(1)}, u32[]{:S(2)}, u32[]{:S(2)}) collective-permute-start(bf16[1,12,32,128]{3,2,1,0:T(8,128)(2,1)S(1)} %get-tuple-element.75), channel_id=1, source_target_pairs={{16,0},{32,16},{48,32},{64,48},{80,64},{96,80},{112,96},{128,112},... | collective-permute-start | bytes 294920 | tf_op jit(solution)/shard_map/ppermute | solution.py:15
  219.6 10.3 %collective-permute-start.6 = (bf16[4,1,32,128]{3,2,1,0:T(8,128)(2,1)S(1)}, bf16[4,1,32,128]{3,2,1,0:T(8,128)(2,1)S(1)}, u32[]{:S(2)}, u32[]{:S(2)}) collective-permute-start(bf16[4,1,32,128]{3,2,1,0:T(8,128)(2,1)S(1)} %get-tuple-element.62), channel_id=1, source_target_pairs={{0,1},{1,2},{2,3},{3,4},{4,5},{5,6},{6,7},{7,8},{8,9},{9,10},{10,1... | collective-permute-start | bytes 98312 | tf_op jit(solution)/shard_map/ppermute | solution.py:14
  222.0 7.9 %collective-permute-start.7 = (bf16[4,1,32,128]{3,2,1,0:T(8,128)(2,1)S(1)}, bf16[4,1,32,128]{3,2,1,0:T(8,128)(2,1)S(1)}, u32[]{:S(2)}, u32[]{:S(2)}) collective-permute-start(bf16[4,1,32,128]{3,2,1,0:T(8,128)(2,1)S(1)} %get-tuple-element.63), channel_id=1, source_target_pairs={{1,0},{2,1},{3,2},{4,3},{5,4},{6,5},{7,6},{8,7},{9,8},{10,9},{11,1... | collective-permute-start | bytes 98312 | tf_op jit(solution)/shard_map/ppermute | solution.py:15
  224.0 120.9 %collective-permute-start.2 = (bf16[4,1,32,128]{3,2,1,0:T(8,128)(2,1)}, bf16[4,1,32,128]{3,2,1,0:T(8,128)(2,1)}, u32[]{:S(2)}, u32[]{:S(2)}) collective-permute-start(bf16[4,1,32,128]{3,2,1,0:T(8,128)(2,1)} %get-tuple-element.66), channel_id=1, source_target_pairs={{0,1},{1,2},{2,3},{3,4},{4,5},{5,6},{6,7},{7,8},{8,9},{9,10},{10,1... | collective-permute-start | bytes 98312 | tf_op jit(solution)/shard_map/ppermute | solution.py:14
  228.5 116.4 %collective-permute-start.3 = (bf16[4,1,32,128]{3,2,1,0:T(8,128)(2,1)}, bf16[4,1,32,128]{3,2,1,0:T(8,128)(2,1)}, u32[]{:S(2)}, u32[]{:S(2)}) collective-permute-start(bf16[4,1,32,128]{3,2,1,0:T(8,128)(2,1)} %get-tuple-element.67), channel_id=1, source_target_pairs={{1,0},{2,1},{3,2},{4,3},{5,4},{6,5},{7,6},{8,7},{9,8},{10,9},{11,1... | collective-permute-start | bytes 98312 | tf_op jit(solution)/shard_map/ppermute | solution.py:15
where the time goes:
time: 352 us; the launch traced here: 351 us
  blocking collectives  307 us (87%)
  starting transfers between devices  25.6 us (7%)
  matrix products  8.36 us (2%)
  other arithmetic  5.1 us (1%)
  local copies, waits for them, and re-layouts  4.14 us (1%)
    psum x1, blocking collectives, on_device(): grad_weight = lax.psum(local_weight, ('gx', 'gy')).astype(jnp.bfloat16)  111 us
    psum x1, blocking collectives, on_device(): lax.psum((jnp.sum(hidden_complete, axis=(0, 1, 2)), jnp.sum(hidden_comple...  101 us
    psum x1, blocking collectives, on_device(): lax.psum((jnp.sum(normed_gradient, axis=(0, 1, 2)), jnp.sum(normed_gradie...  94.6 us
    ppermute x4, starting transfers between devices, padded_2(): before = lax.ppermute(last, axis, up)  15.6 us
    ppermute x4, starting transfers between devices, padded_2(): after = lax.ppermute(first, axis, down)  10.1 us
  transfers between devices with their start and end apart: 8, of which 0 were waited for; matrix products, arithmetic and copies ran while one was open for 3% of the time, Pallas kernels for 0%

commit v1 on v0

v1 whole, which is shorter than its diff:
```python
import functools

import jax
import jax.numpy as jnp
from jax import lax
from jax.experimental import pallas as pl
from jax.experimental.pallas import tpu as pltpu
from jax.sharding import PartitionSpec as P

MESH = pl.DeviceIdType.MESH
F32 = jnp.float32
BF16 = jnp.bfloat16
C = 128
X, Y, Z = 2, 12, 32
COLS = X * Y
VOX = COLS * Z
PLANE = Y * Z
HALF = 14 * C
CORE_T = BF16
YP, ZP, XP = 64, 64, 192
YO, ZO, XO = 0, 8 * YP, 8 * YP + 8 * ZP


def ring(n):
    order = sorted(range(1, n), key=lambda k: -min(k, n - k))
    return order


def kernel(
    total_voxels,
    feat, conv, activ, weight, gain, head, labels, grad_up,
    gin_out, gw_out, gg_out, sg_out,
    fpad, dpad, conv_v, act_v, gu_v, w_v, lab_s, dn_s, dhc_s, ft_s, g_s, gin_v,
    rc, rx, ry, rz,
    core_in, h_s,
    y1, z1, x1, y2, z2, x2, y3, z3, x3, y4, z4, x4, s2y, s2z, s2x, gwbuf,
    lsem, ssem, rsem, hsem, hrsem,
):
    gx, gy = lax.axis_index("gx"), lax.axis_index("gy")
    z, xl, c = gx // 4, (gx // 2) % 2, gx % 2
    xh, y = gy // 8, gy % 8
    x = xh * 2 + xl

    def at_core():
        return (z * 4 + xl * 2 + (1 - c), gy)

    def at_x(j):
        return (z * 4 + (j % 2) * 2 + c, (j // 2) * 8 + y)

    def at_y(j):
        return (gx, xh * 8 + j)

    def at_z(j):
        return (j * 4 + xl * 2 + c, gy)

    up_x, down_x = (gx + 1) % 32, (gx + 31) % 32
    up_y, down_y = (gy + 1) % 16, (gy + 15) % 16

    barrier = pltpu.get_barrier_semaphore()
    partners = [at_core()]
    partners += [at_x((x + k) % 4) for k in ring(4)]
    partners += [at_y((y + k) % 8) for k in ring(8)]
    partners += [at_z((z + k) % 8) for k in ring(8)]
    partners += [(i, j) for i in (down_x, gx, up_x) for j in (down_y, gy, up_y)
                 if not (i is gx and j is gy)]
    for p in partners:
        pl.semaphore_signal(barrier, inc=1, device_id=p, device_id_type=MESH)

    loads = [
        pltpu.make_async_copy(activ, act_v, lsem.at[0]),
        pltpu.make_async_copy(conv, conv_v, lsem.at[1]),
        pltpu.make_async_copy(grad_up, gu_v, lsem.at[2]),
        pltpu.make_async_copy(feat, fpad.at[pl.ds(1, X), pl.ds(1, Y)], lsem.at[3]),
        pltpu.make_async_copy(weight, w_v, lsem.at[4]),
    ]
    for cp in loads:
        cp.start()

    pending = []

    def send(src, dst, sems, rsems, i, dev):
        cp = pltpu.make_async_remote_copy(
            src_ref=src, dst_ref=dst, send_sem=sems.at[i], recv_sem=rsems.at[i],
            device_id=dev, device_id_type=MESH,
        )
        cp.start()
        return cp

    def ring_exchange(stage, n, me, where, src, dst, count):
        for k in ring(n):
            j = (me + k) % n
            send(src(j), dst(me), ssem, rsem, stage, where(j))
        pending.append((stage, count))

    def wait_bytes(sem, ref):
        pltpu.make_async_copy(ref, ref, sem).wait()

    def rim(buf, base):
        inner_x, inner_y = pl.ds(1, X), pl.ds(1, Y)
        moves = [
            (pl.ds(X, 1), inner_y, pl.ds(0, 1), inner_y, (up_x, gy)),
            (pl.ds(1, 1), inner_y, pl.ds(X + 1, 1), inner_y, (down_x, gy)),
            (inner_x, pl.ds(Y, 1), inner_x, pl.ds(0, 1), (gx, up_y)),
            (inner_x, pl.ds(1, 1), inner_x, pl.ds(Y + 1, 1), (gx, down_y)),
            (pl.ds(X, 1), pl.ds(Y, 1), pl.ds(0, 1), pl.ds(0, 1), (up_x, up_y)),
            (pl.ds(X, 1), pl.ds(1, 1), pl.ds(0, 1), pl.ds(Y + 1, 1), (up_x, down_y)),
            (pl.ds(1, 1), pl.ds(Y, 1), pl.ds(X + 1, 1), pl.ds(0, 1), (down_x, up_y)),
            (pl.ds(1, 1), pl.ds(1, 1), pl.ds(X + 1, 1), pl.ds(Y + 1, 1), (down_x, down_y)),
        ]
        return [
            send(buf.at[sx, sy], buf.at[dx, dy], hsem, hrsem, base + i, dev)
            for i, (sx, sy, dx, dy, dev) in enumerate(moves)
        ]

    def clear_rim(buf):
        @pl.when(gx == 0)
        def _():
            buf[0:1] = jnp.zeros((1, Y + 2, Z, C), BF16)

        @pl.when(gx == 31)
        def _():
            buf[X + 1 : X + 2] = jnp.zeros((1, Y + 2, Z, C), BF16)

        @pl.when(gy == 0)
        def _():
            buf[:, 0:1] = jnp.zeros((X + 2, 1, Z, C), BF16)

        @pl.when(gy == 15)
        def _():
            buf[:, Y + 1 : Y + 2] = jnp.zeros((X + 2, 1, Z, C), BF16)

    lab_s[...] = jnp.zeros_like(lab_s)
    for i in range(X):
        lab_s[pl.ds(16 * i, Y), pl.ds(0, Z)] = labels[i].astype(F32)
    lab_t = jnp.transpose(lab_s[...])[0:Z]

    row = lax.broadcasted_iota(jnp.int32, (C, C), 0)
    rep = jnp.zeros((C, C), F32)
    for k in range(3):
        rep = jnp.where(row % 3 == k, head[k : k + 1, :], rep)
    rep = jnp.where(row < 18, rep, 0.0)
    hi = rep.astype(BF16)
    left = rep - hi.astype(F32)
    mid = left.astype(BF16)
    low = (left - mid.astype(F32)).astype(BF16)
    part = row // 3
    back = jnp.where(
        (part == 0) | (part == 3) | (part == 5), hi.astype(F32),
        jnp.where((part == 1) | (part == 4), mid.astype(F32),
                  jnp.where(part == 2, low.astype(F32), 0.0)),
    ).astype(BF16)
    lane = lax.broadcasted_iota(jnp.int32, (C, C), 1)
    lane_class = (lane % 3).astype(F32)

    NT = (((1,), (1,)), ((), ()))

    loads[0].wait()
    loads[1].wait()
    loads[2].wait()
    sums = [jnp.zeros((8, C), F32) for _ in range(4)]
    step = C
    for t in range(VOX // step):
        xi, yi = (4 * t) // Y, (4 * t) % Y
        act = act_v[xi, yi : yi + 4].reshape(step, C)
        logits = (
            lax.dot_general(act, hi, NT, preferred_element_type=F32)
            + lax.dot_general(act, mid, NT, preferred_element_type=F32)
            + lax.dot_general(act, low, NT, preferred_element_type=F32)
        )
        label = jnp.concatenate(
            [jnp.broadcast_to(lab_t[:, 16 * xi + yi + q : 16 * xi + yi + q + 1], (Z, C)) for q in range(4)],
            axis=0,
        )
        dz = 0.5 * (jax.nn.sigmoid(logits) - (label == lane_class).astype(F32))
        dz_hi = dz.astype(BF16).astype(F32)
        dz_left = dz - dz_hi
        dz_mid = dz_left.astype(BF16).astype(F32)
        dz_low = dz_left - dz_mid
        spread = jnp.where(lane < 9, dz_hi, jnp.where(lane < 15, dz_mid, dz_low)).astype(BF16)
        ga = gu_v[xi, yi : yi + 4].reshape(step, C).astype(F32) + jnp.dot(
            spread, back, preferred_element_type=F32
        )
        dn = jnp.where(act.astype(F32) > 0, ga, 0.01 * ga)
        dn_s[pl.ds(t * step, step)] = dn
        h = conv_v[xi, yi : yi + 4].reshape(step, C).astype(F32)
        for i, term in enumerate((h, h * h, dn, dn * h)):
            sums[i] = sums[i] + jnp.sum(term.reshape(step // 8, 8, C), axis=0)
    stats = jnp.concatenate(
        [jnp.sum(s, axis=0, keepdims=True) for s in sums] + [jnp.zeros((4, C), F32)], axis=0
    )

    pl.semaphore_wait(barrier, len(partners))

    rc[c] = stats
    send(rc.at[c], rc.at[c], ssem, rsem, 0, at_core())
    pending.append((0, rc.at[pl.ds(0, 1)]))
    loads[3].wait()
    feat_rim = rim(fpad, 0)
    wait_bytes(rsem.at[0], rc.at[pl.ds(0, 1)])
    stats = rc[0] + rc[1]
    for stage, n, me, where, buf in ((1, 4, x, at_x, rx), (2, 8, y, at_y, ry), (3, 8, z, at_z, rz)):
        buf[me] = stats
        ring_exchange(stage, n, me, where, lambda j: buf.at[me], lambda j: buf.at[j], buf.at[pl.ds(0, n - 1)])
        if stage == 3:
            for cp in feat_rim:
                cp.wait_recv()
            clear_rim(fpad)
            for pln in range(X + 2):
                for b in range(3):
                    block = fpad[pln, b : b + Y].reshape(PLANE, C)
                    ft_s[pl.ds((pln * 3 + b) * C, C)] = jnp.transpose(block)
            loads[4].wait()
        wait_bytes(rsem.at[stage], buf.at[pl.ds(0, n - 1)])
        stats = buf[0]
        for j in range(1, n):
            stats = stats + buf[j]

    mean = stats[0:1] / total_voxels
    rstd = lax.rsqrt(stats[1:2] / total_voxels - mean * mean + 1e-05)
    shift_grad = stats[2:3]
    gain_grad = rstd * (stats[3:4] - mean * shift_grad)
    gg_out[...] = gain_grad
    sg_out[...] = shift_grad
    scale = gain[...] * rstd
    shift_mean = shift_grad / total_voxels
    gain_mean = gain_grad / total_voxels

    zrow = lax.broadcasted_iota(jnp.int32, (step, C), 0) % Z
    for t in range(VOX // step):
        xi, yi = (4 * t) // Y, (4 * t) % Y
        h = conv_v[xi, yi : yi + 4].reshape(step, C).astype(F32)
        dh = scale * (dn_s[pl.ds(t * step, step)] - shift_mean - (h - mean) * rstd * gain_mean)
        mid_dh = dh.astype(BF16)
        dpad[1 + xi, 1 + yi : 5 + yi] = mid_dh.reshape(4, Z, C)
        after = jnp.where(zrow == Z - 1, 0.0, pltpu.roll(dh, step - 1, 0))
        before = jnp.where(zrow == 0, 0.0, pltpu.roll(dh, 1, 0))
        rows = pl.ds(t * step, step)
        dhc_s[rows, 0:C] = after.astype(BF16)
        dhc_s[rows, C : 2 * C] = mid_dh
        dhc_s[rows, 2 * C : 3 * C] = before.astype(BF16)
    dh_rim = rim(dpad, 8)

    for ab in range(9):
        block = jnp.dot(
            ft_s[pl.ds(ab * C, C)], dhc_s[0:PLANE], preferred_element_type=F32
        ) + jnp.dot(
            ft_s[pl.ds((ab + 3) * C, C)], dhc_s[PLANE : 2 * PLANE], preferred_element_type=F32
        )
        for k in range(3):
            g_s[pl.ds((ab * 3 + k) * C, C)] = block[:, k * C : (k + 1) * C].astype(CORE_T)
    g_s[pl.ds(27 * C, C)] = jnp.zeros((C, C), CORE_T)

    mine = pl.multiple_of(c * HALF, HALF)
    others = pl.multiple_of((1 - c) * HALF, HALF)
    send(g_s.at[pl.ds(others, HALF)], core_in, ssem, rsem, 4, at_core())
    pending.append((4, core_in))
    wait_bytes(rsem.at[4], core_in)
    for t in range(14):
        rows = pl.ds(t * C, C)
        h_s[rows] = (
            g_s[pl.ds(pl.multiple_of(mine + t * C, C), C)].astype(F32) + core_in[rows].astype(F32)
        ).astype(BF16)

    def chunk(base, size):
        return lambda j: h_s.at[pl.ds(pl.multiple_of(base + j * size, 64), size)]

    ring_exchange(5, 8, y, at_y, chunk(YO, YP), lambda j: y1.at[j], y1.at[pl.ds(0, 7)])
    ring_exchange(6, 8, z, at_z, chunk(ZO, ZP), lambda j: z1.at[j], z1.at[pl.ds(0, 7)])
    ring_exchange(7, 4, x, at_x, chunk(XO, XP), lambda j: x1.at[j], x1.at[pl.ds(0, 3)])
    y1[y] = h_s[pl.ds(pl.multiple_of(YO + y * YP, YP), YP)]
    z1[z] = h_s[pl.ds(pl.multiple_of(ZO + z * ZP, ZP), ZP)]
    x1[x] = h_s[pl.ds(pl.multiple_of(XO + x * XP, 64), XP)]

    for cp in dh_rim:
        cp.wait_recv()
    clear_rim(dpad)
    for i in range(X):
        total = jnp.zeros((PLANE, 3 * C), F32)
        for ab in range(9):
            a, b = ab // 3, ab % 3
            moved = dpad[i + 2 - a, 2 - b : 2 - b + Y].reshape(PLANE, C)
            total = total + lax.dot_general(
                moved, w_v[pl.ds(ab * 3 * C, 3 * C)], NT, preferred_element_type=F32
            )
        zr = lax.broadcasted_iota(jnp.int32, (PLANE, C), 0) % Z
        minus = jnp.where(zr == Z - 1, 0.0, pltpu.roll(total[:, 0:C], PLANE - 1, 0))
        plus = jnp.where(zr == 0, 0.0, pltpu.roll(total[:, 2 * C : 3 * C], 1, 0))
        gin_v[i] = (total[:, C : 2 * C] + minus + plus).astype(BF16).reshape(Y, Z, C)
    gin_copy = pltpu.make_async_copy(gin_v, gin_out, lsem.at[5])
    gin_copy.start()

    def add_up(buf, n):
        acc = buf[0].astype(F32)
        for j in range(1, n):
            acc = acc + buf[j].astype(F32)
        return acc

    wait_bytes(rsem.at[5], y1.at[pl.ds(0, 7)])
    s2y[...] = add_up(y1, 8).reshape(8, YP // 8, C)
    y2[z] = s2y[z]
    ring_exchange(8, 8, z, at_z, lambda j: s2y.at[j], lambda j: y2.at[j], y2.at[pl.ds(0, 7)])
    wait_bytes(rsem.at[6], z1.at[pl.ds(0, 7)])
    s2z[...] = add_up(z1, 8).reshape(8, ZP // 8, C)
    z2[y] = s2z[y]
    ring_exchange(9, 8, y, at_y, lambda j: s2z.at[j], lambda j: z2.at[j], z2.at[pl.ds(0, 7)])
    wait_bytes(rsem.at[7], x1.at[pl.ds(0, 3)])
    s2x[...] = add_up(x1, 4).reshape(8, XP // 8, C)
    x2[y] = s2x[y]
    ring_exchange(10, 8, y, at_y, lambda j: s2x.at[j], lambda j: x2.at[j], x2.at[pl.ds(0, 7)])

    wait_bytes(rsem.at[10], x2.at[pl.ds(0, 7)])
    x3[z] = add_up(x2, 8)
    ring_exchange(11, 8, z, at_z, lambda j: x3.at[z], lambda j: x3.at[j], x3.at[pl.ds(0, 7)])
    wait_bytes(rsem.at[8], y2.at[pl.ds(0, 7)])
    y3[x] = add_up(y2, 8)
    ring_exchange(12, 4, x, at_x, lambda j: y3.at[x], lambda j: y3.at[j], y3.at[pl.ds(0, 3)])
    wait_bytes(rsem.at[9], z2.at[pl.ds(0, 7)])
    z3[x] = add_up(z2, 8)
    ring_exchange(13, 4, x, at_x, lambda j: z3.at[x], lambda j: z3.at[j], z3.at[pl.ds(0, 3)])

    wait_bytes(rsem.at[12], y3.at[pl.ds(0, 3)])
    y4[z] = add_up(y3, 4)
    ring_exchange(14, 8, z, at_z, lambda j: y4.at[z], lambda j: y4.at[j], y4.at[pl.ds(0, 7)])
    wait_bytes(rsem.at[13], z3.at[pl.ds(0, 3)])
    z4[y] = add_up(z3, 4)
    ring_exchange(15, 8, y, at_y, lambda j: z4.at[y], lambda j: z4.at[j], z4.at[pl.ds(0, 7)])
    wait_bytes(rsem.at[11], x3.at[pl.ds(0, 7)])
    x4[y] = add_up(x3, 8)
    ring_exchange(16, 8, y, at_y, lambda j: x4.at[y], lambda j: x4.at[j], x4.at[pl.ds(0, 7)])

    def place(base, size):
        return lambda j: gwbuf.at[pl.ds(pl.multiple_of(mine + base + j * size, 64), size)]

    wait_bytes(rsem.at[14], y4.at[pl.ds(0, 7)])
    place_y = place(YO, YP)
    place_y(y)[...] = y4[...].reshape(YP, C).astype(BF16)
    ring_exchange(17, 8, y, at_y, lambda j: place_y(y), place_y, gwbuf.at[pl.ds(0, 7 * YP)])
    wait_bytes(rsem.at[15], z4.at[pl.ds(0, 7)])
    place_z = place(ZO, ZP)
    place_z(z)[...] = z4[...].reshape(ZP, C).astype(BF16)
    ring_exchange(18, 8, z, at_z, lambda j: place_z(z), place_z, gwbuf.at[pl.ds(0, 7 * ZP)])
    wait_bytes(rsem.at[16], x4.at[pl.ds(0, 7)])
    place_x = place(XO, XP)
    place_x(x)[...] = x4[...].reshape(XP, C).astype(BF16)
    ring_exchange(19, 4, x, at_x, lambda j: place_x(x), place_x, gwbuf.at[pl.ds(0, 3 * XP)])
    wait_bytes(rsem.at[17], gwbuf.at[pl.ds(0, 7 * YP)])
    wait_bytes(rsem.at[18], gwbuf.at[pl.ds(0, 7 * ZP)])
    wait_bytes(rsem.at[19], gwbuf.at[pl.ds(0, 3 * XP)])

    half = gwbuf.at[pl.ds(mine, HALF)]
    send(half, half, ssem, rsem, 20, at_core())
    pending.append((20, gwbuf.at[pl.ds(0, HALF)]))
    wait_bytes(rsem.at[20], gwbuf.at[pl.ds(0, HALF)])
    gw_copy = pltpu.make_async_copy(gwbuf.at[pl.ds(0, 27 * C)], gw_out, lsem.at[6])
    gw_copy.start()

    for stage, ref in pending:
        wait_bytes(ssem.at[stage], ref)
    for cp in feat_rim + dh_rim:
        cp.wait_send()
    gin_copy.wait()
    gw_copy.wait()


def on_device(feat_in, conv_out, activ, weight, gain, head, labels, grad_up):
    total_voxels = VOX * lax.axis_size("gx") * lax.axis_size("gy") * 1.0
    hbm = pl.BlockSpec(memory_space=pl.ANY)
    vmem = pl.BlockSpec(memory_space=pltpu.VMEM)
    V = pltpu.VMEM
    gin, gw, gg, sg = pl.pallas_call(
        functools.partial(kernel, total_voxels),
        out_shape=(
            jax.ShapeDtypeStruct((X, Y, Z, C), BF16),
            jax.ShapeDtypeStruct((27 * C, C), BF16),
            jax.ShapeDtypeStruct((1, C), F32),
            jax.ShapeDtypeStruct((1, C), F32),
        ),
        in_specs=[hbm, hbm, hbm, hbm, vmem, vmem, vmem, hbm],
        out_specs=(hbm, hbm, vmem, vmem),
        scratch_shapes=[
            V((X + 2, Y + 2, Z, C), BF16),
            V((X + 2, Y + 2, Z, C), BF16),
            V((X, Y, Z, C), BF16),
            V((X, Y, Z, C), BF16),
            V((X, Y, Z, C), BF16),
            V((27 * C, C), BF16),
            V((C, C), F32),
            V((VOX, C), F32),
            V((VOX, 3 * C), BF16),
            V((12 * C, PLANE), BF16),
            V((2 * HALF, C), CORE_T),
            V((X, Y, Z, C), BF16),
            V((2, 8, C), F32), V((4, 8, C), F32), V((8, 8, C), F32), V((8, 8, C), F32),
            V((HALF, C), CORE_T),
            V((HALF, C), BF16),
            V((8, YP, C), BF16), V((8, ZP, C), BF16), V((4, XP, C), BF16),
            V((8, YP // 8, C), F32), V((8, ZP // 8, C), F32), V((8, XP // 8, C), F32),
            V((4, YP // 8, C), F32), V((4, ZP // 8, C), F32), V((8, XP // 8, C), F32),
            V((8, YP // 8, C), F32), V((8, ZP // 8, C), F32), V((8, XP // 8, C), F32),
            V((8, YP // 8, C), F32), V((8, ZP // 8, C), F32), V((8, XP // 8, C), F32),
            V((2 * HALF, C), BF16),
            pltpu.SemaphoreType.DMA((7,)),
            pltpu.SemaphoreType.DMA((21,)),
            pltpu.SemaphoreType.DMA((21,)),
            pltpu.SemaphoreType.DMA((16,)),
            pltpu.SemaphoreType.DMA((16,)),
        ],
        compiler_params=pltpu.CompilerParams(
            collective_id=0, has_side_effects=True, vmem_limit_bytes=48 * 2**20
        ),
        name="conv_block_backward",
    )(feat_in, conv_out, activ, weight, gain.reshape(1, C), head, labels, grad_up)
    return gin, gw, gg.reshape(C), sg.reshape(C)


def solution(mesh):
    return jax.shard_map(
        on_device,
        mesh=mesh,
        in_specs=(
            P("gx", "gy", None, None),
            P("gx", "gy", None, None),
            P("gx", "gy", None, None),
            P(),
            P(),
            P(),
            P("gx", "gy", None),
            P("gx", "gy", None, None),
        ),
        out_specs=(P("gx", "gy", None, None), P(), P(), P()),
        check_vma=False,
    )
```

time: 352 us -> 69 us (0.20)
  blocking collectives: 307 us -> 0 us
  Pallas kernels: 0 us -> 59.8 us
  starting transfers between devices: 25.6 us -> 0 us
  matrix products: 8.36 us -> 0 us
  other arithmetic: 5.1 us -> 0 us
  local copies, waits for them, and re-layouts: 4.14 us -> 8.21 us
    psum x3 -> x0, blocking collectives: 307 us -> none  [the longest x1 111 us: on_device(): grad_weight = lax.psum(local_weight, ('gx', 'gy')).astype(jnp.bfloat16)]
    pallas_call x0 -> x1, Pallas kernels: none -> 59.8 us  [on_device(): pl.pallas_call(functools.partial(kernel, total_voxels), out_shape=(jax.Sh...]
    ppermute x8 -> x0, starting transfers between devices: 25.6 us -> none  [the longest x4 15.6 us: padded_2(): before = lax.ppermute(last, axis, up)]
    dot_general x8 -> x0, matrix products: 8.36 us -> none  [the longest x3 2.56 us: on_device(): jnp.einsum('vko,kio->vi', moved, wgroup, preferred_element_type=jnp.float32)]
    unnamed x44 -> x19, local copies, waits for them, and re-layouts: 1.99 us -> 8.21 us
  transfers between devices with their start and end apart: 8 -> 0, of which waited for: 0 -> 0; matrix products, arithmetic and copies ran while one was open for 3% -> 0% of each run, Pallas kernels for 0% -> 0%
where the time goes in v1:
time: 69 us; the launch traced here: 68.7 us
  Pallas kernels  59.8 us (87%)
  local copies, waits for them, and re-layouts  8.21 us (12%)
    pallas_call x1, Pallas kernels, on_device(): pl.pallas_call(functools.partial(kernel, total_voxels), out_shape=(jax.Sh...  59.8 us
    unnamed x19, local copies, waits for them, and re-layouts  8.21 us

profile of v1, /device:TPU:1, one launch (start us, length us, event | category | flops | bytes accessed | tf_op | source)
XLA Modules:
  0.0 68.7 jit_solution(6310482853879803810)
XLA Ops:
  0.6 0.0 copy-start.5
  0.6 0.0 copy-start.6
  0.7 0.7 %copy.12.labels = s32[2,12,32]{2,1,0:T(8,128)S(1)} copy(s32[2,12,32]{2,0,1:T(2,128)} %param.14) | data formatting | bytes 6144 | tf_op args[6]
  1.4 0.0 copy-done.5
  1.4 0.0 copy-done.6
  1.4 0.0 copy-start
  1.4 1.2 %copy-done = bf16[3456,128]{1,0:T(8,128)(2,1)S(1)} copy-done((bf16[3456,128]{1,0:T(8,128)(2,1)S(1)}, bf16[3456,128]{1,0:T(8,128)(2,1)}, u32[]{:S(2)}) %copy-start) | copy-done | bytes 884760
  2.5 0.0 copy-start.1
  2.5 0.9 %copy-done.1 = bf16[2,12,32,128]{3,2,1,0:T(8,128)(2,1)S(1)} copy-done((bf16[2,12,32,128]{3,2,1,0:T(8,128)(2,1)S(1)}, bf16[2,12,32,128]{3,2,1,0:T(8,128)(2,1)}, u32[]{:S(2)}) %copy-start.1) | copy-done | bytes 196632
  3.5 0.0 copy-start.2
  3.5 0.9 %copy-done.2 = bf16[2,12,32,128]{3,2,1,0:T(8,128)(2,1)S(1)} copy-done((bf16[2,12,32,128]{3,2,1,0:T(8,128)(2,1)S(1)}, bf16[2,12,32,128]{3,2,1,0:T(8,128)(2,1)}, u32[]{:S(2)}) %copy-start.2) | copy-done | bytes 196632
  4.4 0.0 copy-start.3
  4.4 0.9 %copy-done.3 = bf16[2,12,32,128]{3,2,1,0:T(8,128)(2,1)S(1)} copy-done((bf16[2,12,32,128]{3,2,1,0:T(8,128)(2,1)S(1)}, bf16[2,12,32,128]{3,2,1,0:T(8,128)(2,1)}, u32[]{:S(2)}) %copy-start.3) | copy-done | bytes 196632
  5.3 0.0 copy-start.4
  5.3 0.9 %copy-done.4 = bf16[2,12,32,128]{3,2,1,0:T(8,128)(2,1)S(1)} copy-done((bf16[2,12,32,128]{3,2,1,0:T(8,128)(2,1)S(1)}, bf16[2,12,32,128]{3,2,1,0:T(8,128)(2,1)}, u32[]{:S(2)}) %copy-start.4) | copy-done | bytes 196632
  6.3 59.8 %conv_block_backward.1 = (bf16[2,12,32,128]{3,2,1,0:T(8,128)(2,1)S(1)}, bf16[3456,128]{1,0:T(8,128)(2,1)S(1)}, f32[1,128]{1,0:T(1,128)S(1)}, f32[1,128]{1,0:T(1,128)S(1)}) custom-call(bf16[2,12,32,128]{3,2,1,0:T(8,128)(2,1)S(1)} %copy-done.1, bf16[2,12,32,128]{3,2,1,0:T(8,128)(2,1)S(1)} %copy-done.2, bf16[2,12,32,128]{3,2,1,0:T(8,128)(2,1)S(1)} %copy-done.3, ...), custom_call_target="tpu_custom_call" | custom-call | tf_op jit(solution)/shard_map/conv_block_backward/pallas_call | solution.py:370
  66.1 0.7 copy.17
  66.8 0.9 %copy.18 = bf16[3456,128]{1,0:T(8,128)(2,1)} copy(bf16[3456,128]{1,0:T(8,128)(2,1)S(1)} %get-tuple-element.17) | data formatting | bytes 1769472
  67.7 0.5 copy.19
  68.2 0.5 copy.20
Async XLA Ops:
  0.6 0.7 %copy-start.5 = (f32[3,128]{1,0:T(4,128)S(1)}, f32[3,128]{1,0:T(4,128)}, u32[]{:S(2)}) copy-start(f32[3,128]{1,0:T(4,128)} %head.1) | copy-start | bytes 4612
  0.6 0.7 %copy-start.6 = (f32[128]{0:T(128)S(1)}, f32[128]{0:T(128)}, u32[]{:S(2)}) copy-start(f32[128]{0:T(128)} %param.12) | copy-start | bytes 1540
  1.4 1.2 %copy-start = (bf16[3456,128]{1,0:T(8,128)(2,1)S(1)}, bf16[3456,128]{1,0:T(8,128)(2,1)}, u32[]{:S(2)}) copy-start(bf16[3456,128]{1,0:T(8,128)(2,1)} %weight.1) | copy-start | bytes 2654212
  2.5 0.9 %copy-start.1 = (bf16[2,12,32,128]{3,2,1,0:T(8,128)(2,1)S(1)}, bf16[2,12,32,128]{3,2,1,0:T(8,128)(2,1)}, u32[]{:S(2)}) copy-start(bf16[2,12,32,128]{3,2,1,0:T(8,128)(2,1)} %feat.1) | copy-start | bytes 589828
  3.5 0.9 %copy-start.2 = (bf16[2,12,32,128]{3,2,1,0:T(8,128)(2,1)S(1)}, bf16[2,12,32,128]{3,2,1,0:T(8,128)(2,1)}, u32[]{:S(2)}) copy-start(bf16[2,12,32,128]{3,2,1,0:T(8,128)(2,1)} %conv.1) | copy-start | bytes 589828
  4.4 0.9 %copy-start.3 = (bf16[2,12,32,128]{3,2,1,0:T(8,128)(2,1)S(1)}, bf16[2,12,32,128]{3,2,1,0:T(8,128)(2,1)}, u32[]{:S(2)}) copy-start(bf16[2,12,32,128]{3,2,1,0:T(8,128)(2,1)} %activ.1) | copy-start | bytes 589828
  5.3 0.9 %copy-start.4 = (bf16[2,12,32,128]{3,2,1,0:T(8,128)(2,1)S(1)}, bf16[2,12,32,128]{3,2,1,0:T(8,128)(2,1)}, u32[]{:S(2)}) copy-start(bf16[2,12,32,128]{3,2,1,0:T(8,128)(2,1)} %grad_up.1) | copy-start | bytes 589828

commit v2 on v0

v2 whole, which is shorter than its diff:
```python
import functools

import jax
import jax.numpy as jnp
from jax import lax
from jax.experimental import pallas as pl
from jax.experimental.pallas import tpu as pltpu
from jax.sharding import PartitionSpec as P

MESH = pl.DeviceIdType.MESH
F32 = jnp.float32
BF16 = jnp.bfloat16
C = 128
X, Y, Z = 2, 12, 32
COLS = X * Y
VOX = COLS * Z
PLANE = Y * Z
HALF = 14 * C
YP, ZP, XP = 64, 64, 192
YO, ZO, XO = 0, 8 * YP, 8 * YP + 8 * ZP
FULL = 12 * C
NT = (((1,), (1,)), ((), ()))
STATS = 4


def hops(k, n):
    return min(k, n - k)


def ring(n):
    return sorted(range(1, n), key=lambda k: -hops(k, n))


def kernel(
    total_voxels,
    feat, conv, activ, weight, gain, head, labels, grad_up,
    gin_out, gw_out, gg_out, sg_out,
    fpad, dpad, conv_v, dn_v, act_v, gu_v, w_v, lab_s, dhc_s, ft_s, h_s, gin_v,
    ra, rb,
    y1, z1, x1, y2, z2, x2, y3, z3, x3, y4, z4, x4, s2y, s2z, s2x, gwbuf,
    lsem, ssem, rsem,
):
    gx, gy = lax.axis_index("gx"), lax.axis_index("gy")
    z, xl, c = gx // 4, (gx // 2) % 2, gx % 2
    xh, y = gy // 8, gy % 8
    x = xh * 2 + xl

    def at(dx=0, dy=0, dz=0, dc=0):
        ax = (x + dx) % 4
        return (((z + dz) % 8) * 4 + (ax % 2) * 2 + (c + dc) % 2, (ax // 2) * 8 + (y + dy) % 8)

    other = at(dc=1)
    chip = gx // 2
    ahead, behind = (chip + 1) % 16, (chip + 15) % 16
    up_y, down_y = (gy + 1) % 16, (gy + 15) % 16
    up_x, down_x = (gx + 1) % 32, (gx + 31) % 32
    across = c * ahead + (1 - c) * behind

    yc = [(0, k, 0, e) for k in range(8) for e in range(2) if (k, e) != (0, 0)]
    xz = [(j, 0, k, 0) for j in range(4) for k in range(8) if (j, k) != (0, 0)]

    def far_first(offsets):
        return sorted(offsets, key=lambda o: -(hops(o[0], 4) + hops(o[1], 8) + hops(o[2], 8)))

    barrier = pltpu.get_barrier_semaphore()
    partners = [at(*o) for o in far_first(xz) + far_first(yc)]
    partners += [(i, j) for i in (behind * 2 + 1, ahead * 2) for j in (down_y, gy, up_y)]
    partners += [(chip * 2 + e, j) for j in (down_y, up_y) for e in range(2)]
    partners += [(i, j) for i in (down_x, up_x) for j in (down_y, gy, up_y)]
    for p in partners:
        pl.semaphore_signal(barrier, inc=1, device_id=p, device_id_type=MESH)

    own = 2 * c
    loads = [
        pltpu.make_async_copy(activ, act_v, lsem.at[0]),
        pltpu.make_async_copy(grad_up, gu_v, lsem.at[1]),
        pltpu.make_async_copy(conv, conv_v.at[pl.ds(own, X)], lsem.at[2]),
        pltpu.make_async_copy(feat, fpad.at[pl.ds(1 + own, X), pl.ds(1, Y)], lsem.at[3]),
        pltpu.make_async_copy(weight, w_v, lsem.at[4]),
    ]
    for cp in loads:
        cp.start()

    pending = []

    def send(stage, src, dst, dev):
        pltpu.make_async_remote_copy(
            src_ref=src, dst_ref=dst, send_sem=ssem.at[stage], recv_sem=rsem.at[stage],
            device_id=dev, device_id_type=MESH,
        ).start()

    def ring_sends(n, me, axis, src, dst):
        return [
            (hops(k, n), src((me + k) % n), dst(me), at(**{axis: k})) for k in ring(n)
        ]

    def start(stage, sends, count):
        for _, src, dst, dev in sends:
            send(stage, src, dst, dev)
        pending.append((stage, count))

    def wait_bytes(sem, ref):
        pltpu.make_async_copy(ref, ref, sem).wait()

    lab_s[...] = jnp.zeros_like(lab_s)
    for i in range(X):
        lab_s[pl.ds(16 * i, Y), pl.ds(0, Z)] = labels[:, i].astype(F32)
    lab_t = jnp.transpose(lab_s[...])[0:Z]

    row = lax.broadcasted_iota(jnp.int32, (C, C), 0)
    rep = jnp.zeros((C, C), F32)
    for k in range(3):
        rep = jnp.where(row % 3 == k, head[k : k + 1, :], rep)
    rep = jnp.where(row < 18, rep, 0.0)
    hi = rep.astype(BF16)
    left = rep - hi.astype(F32)
    mid = left.astype(BF16)
    low = (left - mid.astype(F32)).astype(BF16)
    part = row // 3
    back = jnp.where(
        (part == 0) | (part == 3) | (part == 5), hi.astype(F32),
        jnp.where((part == 1) | (part == 4), mid.astype(F32),
                  jnp.where(part == 2, low.astype(F32), 0.0)),
    ).astype(BF16)
    lane = lax.broadcasted_iota(jnp.int32, (VOX, C), 1)
    lane_class = (lane % 3).astype(F32)

    loads[0].wait()
    act = act_v[...].reshape(VOX, C)
    logits = (
        lax.dot_general(act, hi, NT, preferred_element_type=F32)
        + lax.dot_general(act, mid, NT, preferred_element_type=F32)
        + lax.dot_general(act, low, NT, preferred_element_type=F32)
    )
    label = jnp.concatenate(
        [
            jnp.broadcast_to(lab_t[:, 16 * i + j : 16 * i + j + 1], (Z, C))
            for i in range(X) for j in range(Y)
        ],
        axis=0,
    )
    dz = 0.5 * (jax.nn.sigmoid(logits) - (label == lane_class).astype(F32))
    dz_hi = dz.astype(BF16).astype(F32)
    dz_left = dz - dz_hi
    dz_mid = dz_left.astype(BF16).astype(F32)
    dz_low = dz_left - dz_mid
    spread = jnp.where(lane < 9, dz_hi, jnp.where(lane < 15, dz_mid, dz_low)).astype(BF16)
    loads[1].wait()
    ga = gu_v[...].reshape(VOX, C).astype(F32) + jnp.dot(
        spread, back, preferred_element_type=F32
    )
    dn = jnp.where(act.astype(F32) > 0, ga, 0.01 * ga)
    dn_v[pl.ds(own, X)] = dn.reshape(X, PLANE, C)
    loads[2].wait()
    h = conv_v[pl.ds(own, X)].reshape(VOX, C).astype(F32)
    stats = jnp.concatenate(
        [
            jnp.sum(jnp.sum(term.reshape(VOX // 8, 8, C), axis=0), axis=0, keepdims=True)
            for term in (h, h * h, dn, dn * h)
        ],
        axis=0,
    )

    slot_a = c * 8 + y
    ra[slot_a] = stats
    pl.semaphore_wait(barrier, len(partners))
    start(0, [(0, ra.at[slot_a], ra.at[slot_a], at(*o)) for o in far_first(yc)], ra.at[pl.ds(0, 15)])

    loads[3].wait()
    inner, edge = pl.ds(1, Y), 1 + own
    near = 1 + own + c
    far = 5 * (1 - c)
    planes = fpad.at[pl.ds(edge, X), inner]
    rim = [(0, planes, planes, other)]
    for e in range(2):
        rim.append((0, fpad.at[near, inner], fpad.at[far, inner], (across * 2 + e, gy)))
        for here, there, dev in ((Y, 0, up_y), (1, Y + 1, down_y)):
            rim.append(
                (0, fpad.at[pl.ds(edge, X), here], fpad.at[pl.ds(edge, X), there], (chip * 2 + e, dev))
            )
            rim.append((0, fpad.at[near, here], fpad.at[far, there], (across * 2 + e, dev)))
    rim_bytes = gwbuf.at[pl.ds(0, (6 * (Y + 2) - COLS) * Z)]
    start(1, rim, rim_bytes)
    mine = conv_v.at[pl.ds(own, X)]
    start(2, [(0, mine, mine, other)], conv_v.at[pl.ds(0, X)])
    mine = dn_v.at[pl.ds(own, X)]
    start(3, [(0, mine, mine, other)], dn_v.at[pl.ds(0, X)])

    wait_bytes(rsem.at[0], ra.at[pl.ds(0, 15)])
    slot_b = x * 8 + z
    rb[slot_b] = jnp.sum(ra[...], axis=0)
    start(4, [(0, rb.at[slot_b], rb.at[slot_b], at(*o)) for o in far_first(xz)], rb.at[pl.ds(0, 31)])

    wait_bytes(rsem.at[1], rim_bytes)

    def clear(cond, ref):
        @pl.when(cond)
        def _():
            ref[...] = jnp.zeros(ref.shape, BF16)

    clear(chip == 0, fpad.at[0])
    clear(chip == 15, fpad.at[5])
    clear(gy == 0, fpad.at[:, 0])
    clear(gy == 15, fpad.at[:, Y + 1])
    for pln in range(6):
        for b in range(3):
            block = jnp.transpose(fpad[pln, b : b + Y].reshape(PLANE, C))
            for a in range(3):
                if 0 <= pln - a < 4:
                    ft_s[(3 * a + b) * C : (3 * a + b + 1) * C, (pln - a) * PLANE : (pln - a + 1) * PLANE] = block
    loads[4].wait()
    wait_bytes(rsem.at[2], conv_v.at[pl.ds(0, X)])
    wait_bytes(rsem.at[3], dn_v.at[pl.ds(0, X)])

    wait_bytes(rsem.at[4], rb.at[pl.ds(0, 31)])
    stats = jnp.sum(rb[...], axis=0)
    mean = stats[0:1] / total_voxels
    rstd = lax.rsqrt(stats[1:2] / total_voxels - mean * mean + 1e-05)
    shift_grad = stats[2:3]
    gain_grad = rstd * (stats[3:4] - mean * shift_grad)
    scale = gain[...] * rstd
    shift_mean = shift_grad / total_voxels
    gain_mean = gain_grad / total_voxels

    zrow = lax.broadcasted_iota(jnp.int32, (PLANE, C), 0) % Z
    for p in range(4):
        hp = conv_v[p].reshape(PLANE, C).astype(F32)
        dh = scale * (dn_v[p] - shift_mean - (hp - mean) * rstd * gain_mean)
        rows = pl.ds(p * PLANE, PLANE)
        after = jnp.where(zrow == Z - 1, 0.0, pltpu.roll(dh, PLANE - 1, 0))
        before = jnp.where(zrow == 0, 0.0, pltpu.roll(dh, 1, 0))
        dhc_s[rows, 0:C] = after.astype(BF16)
        dhc_s[rows, C : 2 * C] = dh.astype(BF16)
        dhc_s[rows, 2 * C : 3 * C] = before.astype(BF16)

    def chunk(base, size):
        return lambda j: h_s.at[pl.ds(pl.multiple_of(base + j * size, 64), size)]

    block = jnp.dot(
        ft_s[pl.ds(pl.multiple_of(c * 7 * C, C), 2 * C)], dhc_s[...], preferred_element_type=F32
    ).astype(BF16)
    for f in range(2):
        for k in range(3):
            h_s[pl.ds((f * 3 + k) * C, C)] = block[f * C : (f + 1) * C, k * C : (k + 1) * C]
    start(5, ring_sends(8, y, "dy", chunk(YO, YP), lambda j: y1.at[j]), y1.at[pl.ds(0, 7)])
    block = jnp.dot(
        ft_s[pl.ds(pl.multiple_of(2 * C + c * 320, 64), 320)], dhc_s[...], preferred_element_type=F32
    ).astype(BF16)
    for j in range(5):
        tail = (1 - c) if j == 4 else (c if j == 0 else 0)
        q = j - c
        for k in range(3):
            at_row = tail * (FULL + k * 64) + (1 - tail) * ((2 + q // 2) * 3 * C + k * C + (q % 2) * 64)
            h_s[pl.ds(pl.multiple_of(at_row, 64), 64)] = block[j * 64 : (j + 1) * 64, k * C : (k + 1) * C]
    h_s[pl.ds(FULL + 192, 64)] = jnp.zeros((64, C), BF16)

    start(6, ring_sends(8, z, "dz", chunk(ZO, ZP), lambda j: z1.at[j]), z1.at[pl.ds(0, 7)])
    start(7, ring_sends(4, x, "dx", chunk(XO, XP), lambda j: x1.at[j]), x1.at[pl.ds(0, 3)])
    y1[y] = chunk(YO, YP)(y)[...]
    z1[z] = chunk(ZO, ZP)(z)[...]
    x1[x] = chunk(XO, XP)(x)[...]
    for i in range(X):
        rows = pl.ds(pl.multiple_of((own + i) * PLANE, PLANE), PLANE)
        dpad[1 + i, 1 : 1 + Y] = dhc_s[rows, C : 2 * C].reshape(Y, Z, C)
    gg_out[...] = gain_grad
    sg_out[...] = shift_grad

    def add_up(buf, n):
        acc = buf[0].astype(F32)
        for j in range(1, n):
            acc = acc + buf[j].astype(F32)
        return acc

    wait_bytes(rsem.at[5], y1.at[pl.ds(0, 7)])
    s2y[...] = add_up(y1, 8).reshape(8, YP // 8, C)
    y2[z] = s2y[z]
    start(8, ring_sends(8, z, "dz", lambda j: s2y.at[j], lambda j: y2.at[j]), y2.at[pl.ds(0, 7)])
    wait_bytes(rsem.at[6], z1.at[pl.ds(0, 7)])
    s2z[...] = add_up(z1, 8).reshape(8, ZP // 8, C)
    z2[y] = s2z[y]
    start(9, ring_sends(8, y, "dy", lambda j: s2z.at[j], lambda j: z2.at[j]), z2.at[pl.ds(0, 7)])
    wait_bytes(rsem.at[7], x1.at[pl.ds(0, 3)])
    s2x[...] = add_up(x1, 4).reshape(8, XP // 8, C)
    x2[y] = s2x[y]
    start(10, ring_sends(8, y, "dy", lambda j: s2x.at[j], lambda j: x2.at[j]), x2.at[pl.ds(0, 7)])

    inner_x = pl.ds(1, X)
    moves = [
        (X, inner, 0, inner, (up_x, gy)),
        (1, inner, X + 1, inner, (down_x, gy)),
        (inner_x, Y, inner_x, 0, (gx, up_y)),
        (inner_x, 1, inner_x, Y + 1, (gx, down_y)),
        (X, Y, 0, 0, (up_x, up_y)),
        (X, 1, 0, Y + 1, (up_x, down_y)),
        (1, Y, X + 1, 0, (down_x, up_y)),
        (1, 1, X + 1, Y + 1, (down_x, down_y)),
    ]
    dh_bytes = gwbuf.at[pl.ds(0, (4 * (Y + 2) - COLS) * Z)]
    start(11, [(0, dpad.at[a, b], dpad.at[d, e], dev) for a, b, d, e, dev in moves], dh_bytes)

    wait_bytes(rsem.at[10], x2.at[pl.ds(0, 7)])
    x3[z] = add_up(x2, 8)
    start(12, ring_sends(8, z, "dz", lambda j: x3.at[z], lambda j: x3.at[j]), x3.at[pl.ds(0, 7)])
    wait_bytes(rsem.at[8], y2.at[pl.ds(0, 7)])
    y3[x] = add_up(y2, 8)
    start(13, ring_sends(4, x, "dx", lambda j: y3.at[x], lambda j: y3.at[j]), y3.at[pl.ds(0, 3)])
    wait_bytes(rsem.at[9], z2.at[pl.ds(0, 7)])
    z3[x] = add_up(z2, 8)
    start(14, ring_sends(4, x, "dx", lambda j: z3.at[x], lambda j: z3.at[j]), z3.at[pl.ds(0, 3)])

    wait_bytes(rsem.at[11], dh_bytes)
    clear(gx == 0, dpad.at[0])
    clear(gx == 31, dpad.at[X + 1])
    clear(gy == 0, dpad.at[:, 0])
    clear(gy == 15, dpad.at[:, Y + 1])
    for i in range(X):
        total = jnp.zeros((PLANE, 3 * C), F32)
        for ab in range(9):
            a, b = ab // 3, ab % 3
            moved = dpad[i + 2 - a, 2 - b : 2 - b + Y].reshape(PLANE, C)
            total = total + lax.dot_general(
                moved, w_v[pl.ds(ab * 3 * C, 3 * C)], NT, preferred_element_type=F32
            )
        minus = jnp.where(zrow == Z - 1, 0.0, pltpu.roll(total[:, 0:C], PLANE - 1, 0))
        plus = jnp.where(zrow == 0, 0.0, pltpu.roll(total[:, 2 * C : 3 * C], 1, 0))
        gin_v[i] = (total[:, C : 2 * C] + minus + plus).astype(BF16).reshape(Y, Z, C)
    gin_copy = pltpu.make_async_copy(gin_v, gin_out, lsem.at[5])
    gin_copy.start()

    wait_bytes(rsem.at[13], y3.at[pl.ds(0, 3)])
    y4[z] = add_up(y3, 4)
    start(15, ring_sends(8, z, "dz", lambda j: y4.at[z], lambda j: y4.at[j]), y4.at[pl.ds(0, 7)])
    wait_bytes(rsem.at[14], z3.at[pl.ds(0, 3)])
    z4[y] = add_up(z3, 4)
    start(16, ring_sends(8, y, "dy", lambda j: z4.at[y], lambda j: z4.at[j]), z4.at[pl.ds(0, 7)])
    wait_bytes(rsem.at[12], x3.at[pl.ds(0, 7)])
    x4[y] = add_up(x3, 8)
    start(17, ring_sends(8, y, "dy", lambda j: x4.at[y], lambda j: x4.at[j]), x4.at[pl.ds(0, 7)])

    half = c * HALF

    def place(base, size):
        return lambda j: gwbuf.at[pl.ds(pl.multiple_of(half + base + j * size, 64), size)]

    place_y, place_z, place_x = place(YO, YP), place(ZO, ZP), place(XO, XP)
    wait_bytes(rsem.at[15], y4.at[pl.ds(0, 7)])
    place_y(y)[...] = y4[...].reshape(YP, C).astype(BF16)
    start(18, ring_sends(8, y, "dy", lambda j: place_y(y), place_y), gwbuf.at[pl.ds(0, 7 * YP)])
    wait_bytes(rsem.at[16], z4.at[pl.ds(0, 7)])
    place_z(z)[...] = z4[...].reshape(ZP, C).astype(BF16)
    start(19, ring_sends(8, z, "dz", lambda j: place_z(z), place_z), gwbuf.at[pl.ds(0, 7 * ZP)])
    wait_bytes(rsem.at[17], x4.at[pl.ds(0, 7)])
    place_x(x)[...] = x4[...].reshape(XP, C).astype(BF16)
    start(20, ring_sends(4, x, "dx", lambda j: place_x(x), place_x), gwbuf.at[pl.ds(0, 3 * XP)])

    parts = (
        (18, 21, 7 * YP, YO, 8 * YP), (19, 22, 7 * ZP, ZO, 8 * ZP), (20, 23, 3 * XP, XO, 4 * XP)
    )
    for stage, onward, arrived, base, size in parts:
        wait_bytes(rsem.at[stage], gwbuf.at[pl.ds(0, arrived)])
        ref = gwbuf.at[pl.ds(pl.multiple_of(half + base, 64), size)]
        start(onward, [(0, ref, ref, other)], gwbuf.at[pl.ds(0, size)])
    for _, onward, _, _, size in parts:
        wait_bytes(rsem.at[onward], gwbuf.at[pl.ds(0, size)])

    outs = [(0, 0, FULL), (HALF, 21 * C, 6 * C), (HALF + 6 * C, 15 * C, 6 * C)]
    for e in range(2):
        for k in range(3):
            outs.append((e * HALF + FULL + k * 64, FULL + k * C + e * 64, 64))
    copies = [
        pltpu.make_async_copy(gwbuf.at[pl.ds(a, n)], gw_out.at[pl.ds(b, n)], lsem.at[6 + i])
        for i, (a, b, n) in enumerate(outs)
    ]
    for cp in copies:
        cp.start()
    for stage, ref in pending:
        wait_bytes(ssem.at[stage], ref)
    gin_copy.wait()
    for cp in copies:
        cp.wait()


def copy_out(*refs):
    n = len(refs) // 3
    ins, outs, held, sem = refs[:n], refs[n : 2 * n], refs[2 * n : 3 * n], refs[-1]
    copies = [pltpu.make_async_copy(ins[i], held[i], sem.at[i]) for i in range(n)]
    for cp in copies:
        cp.start()
    back = [pltpu.make_async_copy(held[i], outs[i], sem.at[n + i]) for i in range(n)]
    for i in range(n):
        copies[i].wait()
        back[i].start()
    for cp in back:
        cp.wait()


def on_device(feat_in, conv_out, activ, weight, gain, head, labels, grad_up):
    total_voxels = VOX * lax.axis_size("gx") * lax.axis_size("gy") * 1.0
    hbm = pl.BlockSpec(memory_space=pltpu.HBM)
    anywhere = pl.BlockSpec(memory_space=pl.ANY)
    vmem = pl.BlockSpec(memory_space=pltpu.VMEM)
    V = pltpu.VMEM
    shapes = (
        jax.ShapeDtypeStruct((X, Y, Z, C), BF16),
        jax.ShapeDtypeStruct((27 * C, C), BF16),
        jax.ShapeDtypeStruct((1, C), F32),
        jax.ShapeDtypeStruct((1, C), F32),
    )
    outs = pl.pallas_call(
        functools.partial(kernel, total_voxels),
        out_shape=shapes,
        in_specs=[hbm, hbm, hbm, hbm, vmem, vmem, vmem, hbm],
        out_specs=(anywhere, anywhere, vmem, vmem),
        scratch_shapes=[
            V((6, Y + 2, Z, C), BF16),
            V((X + 2, Y + 2, Z, C), BF16),
            V((4, Y, Z, C), BF16),
            V((4, PLANE, C), F32),
            V((X, Y, Z, C), BF16),
            V((X, Y, Z, C), BF16),
            V((27 * C, C), BF16),
            V((C, C), F32),
            V((4 * PLANE, 3 * C), BF16),
            V((9 * C, 4 * PLANE), BF16),
            V((HALF, C), BF16),
            V((X, Y, Z, C), BF16),
            V((16, STATS, C), F32), V((32, STATS, C), F32),
            V((8, YP, C), BF16), V((8, ZP, C), BF16), V((4, XP, C), BF16),
            V((8, YP // 8, C), F32), V((8, ZP // 8, C), F32), V((8, XP // 8, C), F32),
            V((4, YP // 8, C), F32), V((4, ZP // 8, C), F32), V((8, XP // 8, C), F32),
            V((8, YP // 8, C), F32), V((8, ZP // 8, C), F32), V((8, XP // 8, C), F32),
            V((8, YP // 8, C), F32), V((8, ZP // 8, C), F32), V((8, XP // 8, C), F32),
            V((2 * HALF, C), BF16),
            pltpu.SemaphoreType.DMA((15,)),
            pltpu.SemaphoreType.DMA((24,)),
            pltpu.SemaphoreType.DMA((24,)),
        ],
        compiler_params=pltpu.CompilerParams(
            collective_id=0, has_side_effects=True, vmem_limit_bytes=58 * 2**20
        ),
        name="conv_block_backward",
    )(feat_in, conv_out, activ, weight, gain.reshape(1, C), head, labels.transpose(1, 0, 2), grad_up)
    gin, gw, gg, sg = pl.pallas_call(
        copy_out,
        out_shape=shapes,
        in_specs=[anywhere] * 4,
        out_specs=(hbm,) * 4,
        scratch_shapes=[V(t.shape, t.dtype) for t in shapes] + [pltpu.SemaphoreType.DMA((8,))],
        compiler_params=pltpu.CompilerParams(vmem_limit_bytes=60 * 2**20),
        name="copy_outputs",
    )(*outs)
    return gin, gw, gg.reshape(C), sg.reshape(C)


def solution(mesh):
    return jax.shard_map(
        on_device,
        mesh=mesh,
        in_specs=(
            P("gx", "gy", None, None),
            P("gx", "gy", None, None),
            P("gx", "gy", None, None),
            P(),
            P(),
            P(),
            P("gx", "gy", None),
            P("gx", "gy", None, None),
        ),
        out_specs=(P("gx", "gy", None, None), P(), P(), P()),
        check_vma=False,
    )
```

time: 352 us -> 60.3 us (0.17)
  blocking collectives: 307 us -> 0 us
  Pallas kernels: 0 us -> 59.5 us
  starting transfers between devices: 25.6 us -> 0 us
  matrix products: 8.36 us -> 0 us
  other arithmetic: 5.1 us -> 0 us
  local copies, waits for them, and re-layouts: 4.14 us -> 0 us
    psum x3 -> x0, blocking collectives: 307 us -> none  [the longest x1 111 us: on_device(): grad_weight = lax.psum(local_weight, ('gx', 'gy')).astype(jnp.bfloat16)]
    pallas_call x0 -> x2, Pallas kernels: none -> 59.5 us  [the longest x1 57.2 us: on_device(): pl.pallas_call(functools.partial(kernel, total_voxels), out_shape=shapes,...]
    ppermute x8 -> x0, starting transfers between devices: 25.6 us -> none  [the longest x4 15.6 us: padded_2(): before = lax.ppermute(last, axis, up)]
    dot_general x8 -> x0, matrix products: 8.36 us -> none  [the longest x3 2.56 us: on_device(): jnp.einsum('vko,kio->vi', moved, wgroup, preferred_element_type=jnp.float32)]
  transfers between devices with their start and end apart: 8 -> 0, of which waited for: 0 -> 0; matrix products, arithmetic and copies ran while one was open for 3% -> 0% of each run, Pallas kernels for 0% -> 0%
where the time goes in v2:
time: 60.3 us; the launch traced here: 60.1 us
  Pallas kernels  59.5 us (99%)
  between operations  0.64 us (1%)
    pallas_call x1, Pallas kernels, on_device(): pl.pallas_call(functools.partial(kernel, total_voxels), out_shape=shapes,...  57.2 us
    pallas_call x1, Pallas kernels, on_device(): pl.pallas_call(copy_out, out_shape=shapes, in_specs=[anywhere] * 4, out_s...  2.26 us

profile of v2, /device:TPU:1, one launch (start us, length us, event | category | flops | bytes accessed | tf_op | source)
XLA Modules:
  0.0 60.1 jit_solution(3355661437831391465)
XLA Ops:
  0.6 57.2 %conv_block_backward.1 = (bf16[2,12,32,128]{3,2,1,0:T(8,128)(2,1)}, bf16[3456,128]{1,0:T(8,128)(2,1)}, f32[1,128]{1,0:T(1,128)}, f32[1,128]{1,0:T(1,128)}) custom-call(bf16[2,12,32,128]{3,2,1,0:T(8,128)(2,1)} %feat.1, bf16[2,12,32,128]{3,2,1,0:T(8,128)(2,1)} %conv.1, bf16[2,12,32,128]{3,2,1,0:T(8,128)(2,1)} %activ.1, bf16[3456,128]{1,0:T(8,128)(2,1)} %weight.1, ...), custom_call_target="tpu_custom_call" | custom-call | tf_op jit(solution)/shard_map/conv_block_backward/pallas_call | solution.py:409
  57.9 2.3 %copy_outputs.1 = (bf16[2,12,32,128]{3,2,1,0:T(8,128)(2,1)}, bf16[3456,128]{1,0:T(8,128)(2,1)}, f32[1,128]{1,0:T(1,128)}, f32[1,128]{1,0:T(1,128)}) custom-call(bf16[2,12,32,128]{3,2,1,0:T(8,128)(2,1)} %get-tuple-element.12.refs_0_, bf16[3456,128]{1,0:T(8,128)(2,1)} %get-tuple-element.13.refs_1_, f32[1,128]{1,0:T(1,128)} %get-tuple-element.14.refs_2_, ...), custom_call_target="tpu_custom_call" | custom-call | tf_op jit(solution)/shard_map/copy_outputs/pallas_call | solution.py:443

commit v3 on v2

--- a/solution.py
+++ b/solution.py
@@ -33,12 +33,12 @@
 
 def kernel(
     total_voxels,
-    feat, conv, activ, weight, gain, head, labels, grad_up,
+    feat, conv, activ, weight, gain_in, head_in, labels_in, grad_up,
     gin_out, gw_out, gg_out, sg_out,
-    fpad, dpad, conv_v, dn_v, act_v, gu_v, w_v, lab_s, dhc_s, ft_s, h_s, gin_v,
+    gain, head, labels, fpad, dpad, conv_v, dn_v, act_v, gu_v, w_v, lab_s, dhc_s, ft_s, h_s,
     ra, rb,
     y1, z1, x1, y2, z2, x2, y3, z3, x3, y4, z4, x4, s2y, s2z, s2x, gwbuf,
-    lsem, ssem, rsem,
+    lsem, ssem, rsem, gsem,
 ):
     gx, gy = lax.axis_index("gx"), lax.axis_index("gy")
     z, xl, c = gx // 4, (gx // 2) % 2, gx % 2
@@ -61,6 +61,22 @@
 
     def far_first(offsets):
         return sorted(offsets, key=lambda o: -(hops(o[0], 4) + hops(o[1], 8) + hops(o[2], 8)))
+
+    own = 2 * c
+    small = [
+        pltpu.make_async_copy(labels_in, labels, lsem.at[6]),
+        pltpu.make_async_copy(head_in, head, lsem.at[7]),
+        pltpu.make_async_copy(gain_in, gain, lsem.at[8]),
+    ]
+    loads = [
+        pltpu.make_async_copy(activ, act_v, lsem.at[0]),
+        pltpu.make_async_copy(grad_up, gu_v, lsem.at[1]),
+        pltpu.make_async_copy(conv, conv_v.at[pl.ds(own, X)], lsem.at[2]),
+        pltpu.make_async_copy(feat, fpad.at[pl.ds(1 + own, X), pl.ds(1, Y)], lsem.at[3]),
+        pltpu.make_async_copy(weight, w_v, lsem.at[4]),
+    ]
+    for cp in small + loads:
+        cp.start()
 
     barrier = pltpu.get_barrier_semaphore()
     partners = [at(*o) for o in far_first(xz) + far_first(yc)]
@@ -70,22 +86,12 @@
     for p in partners:
         pl.semaphore_signal(barrier, inc=1, device_id=p, device_id_type=MESH)
 
-    own = 2 * c
-    loads = [
-        pltpu.make_async_copy(activ, act_v, lsem.at[0]),
-        pltpu.make_async_copy(grad_up, gu_v, lsem.at[1]),
-        pltpu.make_async_copy(conv, conv_v.at[pl.ds(own, X)], lsem.at[2]),
-        pltpu.make_async_copy(feat, fpad.at[pl.ds(1 + own, X), pl.ds(1, Y)], lsem.at[3]),
-        pltpu.make_async_copy(weight, w_v, lsem.at[4]),
-    ]
-    for cp in loads:
-        cp.start()
-
     pending = []
 
-    def send(stage, src, dst, dev):
+    def send(stage, src, dst, dev, arrival=None):
         pltpu.make_async_remote_copy(
-            src_ref=src, dst_ref=dst, send_sem=ssem.at[stage], recv_sem=rsem.at[stage],
+            src_ref=src, dst_ref=dst, send_sem=ssem.at[stage],
+            recv_sem=rsem.at[stage] if arrival is None else arrival,
             device_id=dev, device_id_type=MESH,
         ).start()
 
@@ -101,6 +107,9 @@
 
     def wait_bytes(sem, ref):
         pltpu.make_async_copy(ref, ref, sem).wait()
+
+    for cp in small:
+        cp.wait()
 
     lab_s[...] = jnp.zeros_like(lab_s)
     for i in range(X):
@@ -122,7 +131,7 @@
         jnp.where((part == 1) | (part == 4), mid.astype(F32),
                   jnp.where(part == 2, low.astype(F32), 0.0)),
     ).astype(BF16)
-    lane = lax.broadcasted_iota(jnp.int32, (VOX, C), 1)
+    lane = lax.broadcasted_iota(jnp.int32, (1, C), 1)
     lane_class = (lane % 3).astype(F32)
 
     loads[0].wait()
@@ -222,7 +231,7 @@
     shift_mean = shift_grad / total_voxels
     gain_mean = gain_grad / total_voxels
 
-    zrow = lax.broadcasted_iota(jnp.int32, (PLANE, C), 0) % Z
+    zrow = lax.broadcasted_iota(jnp.int32, (PLANE, C), 0) & (Z - 1)
     for p in range(4):
         hp = conv_v[p].reshape(PLANE, C).astype(F32)
         dh = scale * (dn_v[p] - shift_mean - (hp - mean) * rstd * gain_mean)
@@ -237,24 +246,28 @@
         return lambda j: h_s.at[pl.ds(pl.multiple_of(base + j * size, 64), size)]
 
     block = jnp.dot(
-        ft_s[pl.ds(pl.multiple_of(c * 7 * C, C), 2 * C)], dhc_s[...], preferred_element_type=F32
+        ft_s[pl.ds(pl.multiple_of(c * 6 * C, C), 3 * C)], dhc_s[...], preferred_element_type=F32
     ).astype(BF16)
-    for f in range(2):
+    for f in range(3):
         for k in range(3):
             h_s[pl.ds((f * 3 + k) * C, C)] = block[f * C : (f + 1) * C, k * C : (k + 1) * C]
-    start(5, ring_sends(8, y, "dy", chunk(YO, YP), lambda j: y1.at[j]), y1.at[pl.ds(0, 7)])
+    first = ring_sends(8, y, "dy", chunk(YO, YP), lambda j: y1.at[j])
+    second = ring_sends(8, z, "dz", chunk(ZO, ZP), lambda j: z1.at[j])
+    for sy, sz in zip(first, second):
+        send(5, *sy[1:])
+        send(6, *sz[1:])
+    pending.append((5, y1.at[pl.ds(0, 7)]))
+    pending.append((6, z1.at[pl.ds(0, 7)]))
     block = jnp.dot(
-        ft_s[pl.ds(pl.multiple_of(2 * C + c * 320, 64), 320)], dhc_s[...], preferred_element_type=F32
+        ft_s[pl.ds(pl.multiple_of(3 * C + c * 192, 64), 192)], dhc_s[...], preferred_element_type=F32
     ).astype(BF16)
-    for j in range(5):
-        tail = (1 - c) if j == 4 else (c if j == 0 else 0)
-        q = j - c
+    for j in range(3):
+        tail = (1 - c) if j == 2 else (c if j == 0 else 0)
         for k in range(3):
-            at_row = tail * (FULL + k * 64) + (1 - tail) * ((2 + q // 2) * 3 * C + k * C + (q % 2) * 64)
+            at_row = tail * (FULL + k * 64) + (1 - tail) * (9 * C + k * C + (j - c) * 64)
             h_s[pl.ds(pl.multiple_of(at_row, 64), 64)] = block[j * 64 : (j + 1) * 64, k * C : (k + 1) * C]
     h_s[pl.ds(FULL + 192, 64)] = jnp.zeros((64, C), BF16)
 
-    start(6, ring_sends(8, z, "dz", chunk(ZO, ZP), lambda j: z1.at[j]), z1.at[pl.ds(0, 7)])
     start(7, ring_sends(4, x, "dx", chunk(XO, XP), lambda j: x1.at[j]), x1.at[pl.ds(0, 3)])
     y1[y] = chunk(YO, YP)(y)[...]
     z1[z] = chunk(ZO, ZP)(z)[...]
@@ -323,9 +336,7 @@
             )
         minus = jnp.where(zrow == Z - 1, 0.0, pltpu.roll(total[:, 0:C], PLANE - 1, 0))
         plus = jnp.where(zrow == 0, 0.0, pltpu.roll(total[:, 2 * C : 3 * C], 1, 0))
-        gin_v[i] = (total[:, C : 2 * C] + minus + plus).astype(BF16).reshape(Y, Z, C)
-    gin_copy = pltpu.make_async_copy(gin_v, gin_out, lsem.at[5])
-    gin_copy.start()
+        gin_out[i] = (total[:, C : 2 * C] + minus + plus).astype(BF16).reshape(Y, Z, C)
 
     wait_bytes(rsem.at[13], y3.at[pl.ds(0, 3)])
     y4[z] = add_up(y3, 4)
@@ -337,60 +348,56 @@
     x4[y] = add_up(x3, 8)
     start(17, ring_sends(8, y, "dy", lambda j: x4.at[y], lambda j: x4.at[j]), x4.at[pl.ds(0, 7)])
 
-    half = c * HALF
-
-    def place(base, size):
-        return lambda j: gwbuf.at[pl.ds(pl.multiple_of(half + base + j * size, 64), size)]
-
-    place_y, place_z, place_x = place(YO, YP), place(ZO, ZP), place(XO, XP)
-    wait_bytes(rsem.at[15], y4.at[pl.ds(0, 7)])
-    place_y(y)[...] = y4[...].reshape(YP, C).astype(BF16)
-    start(18, ring_sends(8, y, "dy", lambda j: place_y(y), place_y), gwbuf.at[pl.ds(0, 7 * YP)])
-    wait_bytes(rsem.at[16], z4.at[pl.ds(0, 7)])
-    place_z(z)[...] = z4[...].reshape(ZP, C).astype(BF16)
-    start(19, ring_sends(8, z, "dz", lambda j: place_z(z), place_z), gwbuf.at[pl.ds(0, 7 * ZP)])
-    wait_bytes(rsem.at[17], x4.at[pl.ds(0, 7)])
-    place_x(x)[...] = x4[...].reshape(XP, C).astype(BF16)
-    start(20, ring_sends(4, x, "dx", lambda j: place_x(x), place_x), gwbuf.at[pl.ds(0, 3 * XP)])
-
-    parts = (
-        (18, 21, 7 * YP, YO, 8 * YP), (19, 22, 7 * ZP, ZO, 8 * ZP), (20, 23, 3 * XP, XO, 4 * XP)
-    )
-    for stage, onward, arrived, base, size in parts:
-        wait_bytes(rsem.at[stage], gwbuf.at[pl.ds(0, arrived)])
-        ref = gwbuf.at[pl.ds(pl.multiple_of(half + base, 64), size)]
-        start(onward, [(0, ref, ref, other)], gwbuf.at[pl.ds(0, size)])
-    for _, onward, _, _, size in parts:
-        wait_bytes(rsem.at[onward], gwbuf.at[pl.ds(0, size)])
-
-    outs = [(0, 0, FULL), (HALF, 21 * C, 6 * C), (HALF + 6 * C, 15 * C, 6 * C)]
-    for e in range(2):
-        for k in range(3):
-            outs.append((e * HALF + FULL + k * 64, FULL + k * C + e * 64, 64))
-    copies = [
-        pltpu.make_async_copy(gwbuf.at[pl.ds(a, n)], gw_out.at[pl.ds(b, n)], lsem.at[6 + i])
-        for i, (a, b, n) in enumerate(outs)
-    ]
+    half, half_other = c * HALF, (1 - c) * HALF
+    spans = (
+        (15, y4, 18, 21, 8, y, "dy", YO, YP), (16, z4, 19, 22, 8, z, "dz", ZO, ZP),
+        (17, x4, 20, 23, 4, x, "dx", XO, XP),
+    )
+
+    def place(base, j, size):
+        return gwbuf.at[pl.ds(pl.multiple_of(half + base + j * size, 64), size)]
+
+    for stage, buf, out, onward, n, me, axis, base, size in spans:
+        wait_bytes(rsem.at[stage], buf.at[pl.ds(0, 7)])
+        ref = place(base, me, size)
+        ref[...] = buf[...].reshape(size, C).astype(BF16)
+        for k in ring(n):
+            send(out, ref, ref, at(**{axis: k}), gsem.at[out - 18, k])
+        pending.append((out, gwbuf.at[pl.ds(0, (n - 1) * size)]))
+    for stage, buf, out, onward, n, me, axis, base, size in spans:
+        ref = place(base, me, size)
+        send(onward, ref, ref, other)
+        pending.append((onward, gwbuf.at[pl.ds(0, n * size)]))
+    for far in range(1, 5):
+        for stage, buf, out, onward, n, me, axis, base, size in spans:
+            for k in range(1, n):
+                if hops(k, n) == far:
+                    ref = place(base, (me - k) % n, size)
+                    wait_bytes(gsem.at[out - 18, k], ref)
+                    send(onward, ref, ref, other)
+
+    def write_half(core, base):
+        moves = [(t * C, core * 18 * C + t * C, C) for t in range(9)]
+        moves += [(t * C, core * 6 * C + t * C, C) for t in range(9, 12)]
+        moves += [(FULL + k * 64, FULL + k * C + core * 64, 64) for k in range(3)]
+        for src, dst, n in moves:
+            gw_out[pl.ds(pl.multiple_of(dst, 64), n)] = gwbuf[pl.ds(pl.multiple_of(base + src, 64), n)]
+
+    write_half(c, half)
+    for _, _, _, onward, n, _, _, _, size in spans:
+        wait_bytes(rsem.at[onward], gwbuf.at[pl.ds(0, n * size)])
+    write_half(1 - c, half_other)
+    for stage, ref in pending:
+        wait_bytes(ssem.at[stage], ref)
+
+
+def copy_out(*refs):
+    n = len(refs) // 2
+    ins, outs, sem = refs[:n], refs[n : 2 * n], refs[-1]
+    copies = [pltpu.make_async_copy(ins[i], outs[i], sem.at[i]) for i in range(n)]
     for cp in copies:
         cp.start()
-    for stage, ref in pending:
-        wait_bytes(ssem.at[stage], ref)
-    gin_copy.wait()
     for cp in copies:
-        cp.wait()
-
-
-def copy_out(*refs):
-    n = len(refs) // 3
-    ins, outs, held, sem = refs[:n], refs[n : 2 * n], refs[2 * n : 3 * n], refs[-1]
-    copies = [pltpu.make_async_copy(ins[i], held[i], sem.at[i]) for i in range(n)]
-    for cp in copies:
-        cp.start()
-    back = [pltpu.make_async_copy(held[i], outs[i], sem.at[n + i]) for i in range(n)]
-    for i in range(n):
-        copies[i].wait()
-        back[i].start()
-    for cp in back:
         cp.wait()
 
 
@@ -406,12 +413,19 @@
         jax.ShapeDtypeStruct((1, C), F32),
         jax.ShapeDtypeStruct((1, C), F32),
     )
+    operands = (
+        feat_in, conv_out, activ, weight, gain.reshape(1, C), head, labels.transpose(1, 0, 2), grad_up
+    )
+    operands = [pltpu.with_memory_space_constraint(t, pltpu.HBM) for t in operands]
     outs = pl.pallas_call(
         functools.partial(kernel, total_voxels),
         out_shape=shapes,
-        in_specs=[hbm, hbm, hbm, hbm, vmem, vmem, vmem, hbm],
-        out_specs=(anywhere, anywhere, vmem, vmem),
+        in_specs=[hbm] * 8,
+        out_specs=(vmem,) * 4,
         scratch_shapes=[
+            V((1, C), F32),
+            V((3, C), F32),
+            V((Y, X, Z), jnp.int32),
             V((6, Y + 2, Z, C), BF16),
             V((X + 2, Y + 2, Z, C), BF16),
             V((4, Y, Z, C), BF16),
@@ -423,7 +437,6 @@
             V((4 * PLANE, 3 * C), BF16),
             V((9 * C, 4 * PLANE), BF16),
             V((HALF, C), BF16),
-            V((X, Y, Z, C), BF16),
             V((16, STATS, C), F32), V((32, STATS, C), F32),
             V((8, YP, C), BF16), V((8, ZP, C), BF16), V((4, XP, C), BF16),
             V((8, YP // 8, C), F32), V((8, ZP // 8, C), F32), V((8, XP // 8, C), F32),
@@ -431,22 +444,23 @@
             V((8, YP // 8, C), F32), V((8, ZP // 8, C), F32), V((8, XP // 8, C), F32),
             V((8, YP // 8, C), F32), V((8, ZP // 8, C), F32), V((8, XP // 8, C), F32),
             V((2 * HALF, C), BF16),
-            pltpu.SemaphoreType.DMA((15,)),
+            pltpu.SemaphoreType.DMA((9,)),
             pltpu.SemaphoreType.DMA((24,)),
             pltpu.SemaphoreType.DMA((24,)),
+            pltpu.SemaphoreType.DMA((3, 8)),
         ],
         compiler_params=pltpu.CompilerParams(
-            collective_id=0, has_side_effects=True, vmem_limit_bytes=58 * 2**20
+            collective_id=0, has_side_effects=True, vmem_limit_bytes=40 * 2**20
         ),
         name="conv_block_backward",
-    )(feat_in, conv_out, activ, weight, gain.reshape(1, C), head, labels.transpose(1, 0, 2), grad_up)
+    )(*operands)
     gin, gw, gg, sg = pl.pallas_call(
         copy_out,
         out_shape=shapes,
         in_specs=[anywhere] * 4,
         out_specs=(hbm,) * 4,
-        scratch_shapes=[V(t.shape, t.dtype) for t in shapes] + [pltpu.SemaphoreType.DMA((8,))],
-        compiler_params=pltpu.CompilerParams(vmem_limit_bytes=60 * 2**20),
+        scratch_shapes=[pltpu.SemaphoreType.DMA((4,))],
+        compiler_params=pltpu.CompilerParams(vmem_limit_bytes=4 * 2**20),
         name="copy_outputs",
     )(*outs)
     return gin, gw, gg.reshape(C), sg.reshape(C)

time: 60.3 us -> 56.2 us (0.932)
  Pallas kernels: 59.5 us -> 55.4 us
    pallas_call x1, Pallas kernels: 57.2 us -> 54.4 us  [on_device(): pl.pallas_call(functools.partial(kernel, total_voxels), out_shape=shapes,...]
    pallas_call x1, Pallas kernels: 2.26 us -> 1.02 us  [on_device(): pl.pallas_call(copy_out, out_shape=shapes, in_specs=[anywhere] * 4, out_s...]
where the time goes in v3:
time: 56.2 us; the launch traced here: 56.1 us
  Pallas kernels  55.4 us (99%)
  between operations  0.64 us (1%)
    pallas_call x1, Pallas kernels, on_device(): pl.pallas_call(functools.partial(kernel, total_voxels), out_shape=shapes,...  54.4 us

profile of v3, /device:TPU:1, one launch (start us, length us, event | category | flops | bytes accessed | tf_op | source)
XLA Modules:
  0.0 56.1 jit_solution(7091052904840832664)
XLA Ops:
  0.6 54.4 %conv_block_backward.1 = (bf16[2,12,32,128]{3,2,1,0:T(8,128)(2,1)S(1)}, bf16[3456,128]{1,0:T(8,128)(2,1)S(1)}, f32[1,128]{1,0:T(1,128)S(1)}, f32[1,128]{1,0:T(1,128)S(1)}) custom-call(bf16[2,12,32,128]{3,2,1,0:T(8,128)(2,1)} %feat.1, bf16[2,12,32,128]{3,2,1,0:T(8,128)(2,1)} %conv.1, bf16[2,12,32,128]{3,2,1,0:T(8,128)(2,1)} %activ.1, ...), custom_call_target="tpu_custom_call" | custom-call | tf_op jit(solution)/shard_map/conv_block_backward/pallas_call | solution.py:420
  55.1 1.0 %copy_outputs.1 = (bf16[2,12,32,128]{3,2,1,0:T(8,128)(2,1)}, bf16[3456,128]{1,0:T(8,128)(2,1)}, f32[1,128]{1,0:T(1,128)}, f32[1,128]{1,0:T(1,128)}) custom-call(bf16[2,12,32,128]{3,2,1,0:T(8,128)(2,1)S(1)} %get-tuple-element.12.refs_0_, bf16[3456,128]{1,0:T(8,128)(2,1)S(1)} %get-tuple-element.13.refs_1_, f32[1,128]{1,0:T(1,128)S(1)} %get-tuple-element.14.refs_2_, ...), custom_call_target="tpu_custom_call" | custom-call | tf_op jit(solution)/shard_map/copy_outputs/pallas_call | solution.py:457

commit v4 on v3

--- a/solution.py
+++ b/solution.py
@@ -38,7 +38,7 @@
     gain, head, labels, fpad, dpad, conv_v, dn_v, act_v, gu_v, w_v, lab_s, dhc_s, ft_s, h_s,
     ra, rb,
     y1, z1, x1, y2, z2, x2, y3, z3, x3, y4, z4, x4, s2y, s2z, s2x, gwbuf,
-    lsem, ssem, rsem, gsem,
+    lsem, ssem, rsem, late,
 ):
     gx, gy = lax.axis_index("gx"), lax.axis_index("gy")
     z, xl, c = gx // 4, (gx // 2) % 2, gx % 2
@@ -61,6 +61,23 @@
 
     def far_first(offsets):
         return sorted(offsets, key=lambda o: -(hops(o[0], 4) + hops(o[1], 8) + hops(o[2], 8)))
+
+    barrier = pltpu.get_barrier_semaphore()
+
+    def signal(sem, dev):
+        pl.semaphore_signal(sem, inc=1, device_id=dev, device_id_type=MESH)
+
+    rank = z * 4 + x
+
+    def rank_of(o):
+        return ((z + o[2]) % 8) * 4 + (x + o[0]) % 4
+
+    partners = [at(*o) for o in far_first(yc)]
+    partners += [(i, j) for i in (behind * 2 + 1, ahead * 2) for j in (down_y, gy, up_y)]
+    partners += [(chip * 2 + e, j) for j in (down_y, up_y) for e in range(2)]
+    partners += [(i, j) for i in (down_x, up_x) for j in (down_y, gy, up_y)]
+    for p in partners[:15]:
+        signal(barrier, p)
 
     own = 2 * c
     small = [
@@ -78,20 +95,18 @@
     for cp in small + loads:
         cp.start()
 
-    barrier = pltpu.get_barrier_semaphore()
-    partners = [at(*o) for o in far_first(xz) + far_first(yc)]
-    partners += [(i, j) for i in (behind * 2 + 1, ahead * 2) for j in (down_y, gy, up_y)]
-    partners += [(chip * 2 + e, j) for j in (down_y, up_y) for e in range(2)]
-    partners += [(i, j) for i in (down_x, up_x) for j in (down_y, gy, up_y)]
-    for p in partners:
-        pl.semaphore_signal(barrier, inc=1, device_id=p, device_id_type=MESH)
+    for p in partners[15:]:
+        signal(barrier, p)
+    for o in far_first(xz):
+        @pl.when(rank_of(o) > rank)
+        def _():
+            signal(barrier, at(*o))
 
     pending = []
 
-    def send(stage, src, dst, dev, arrival=None):
+    def send(stage, src, dst, dev):
         pltpu.make_async_remote_copy(
-            src_ref=src, dst_ref=dst, send_sem=ssem.at[stage],
-            recv_sem=rsem.at[stage] if arrival is None else arrival,
+            src_ref=src, dst_ref=dst, send_sem=ssem.at[stage], recv_sem=rsem.at[stage],
             device_id=dev, device_id_type=MESH,
         ).start()
 
@@ -172,8 +187,13 @@
 
     slot_a = c * 8 + y
     ra[slot_a] = stats
-    pl.semaphore_wait(barrier, len(partners))
+    pl.semaphore_wait(barrier, len(partners) + rank)
     start(0, [(0, ra.at[slot_a], ra.at[slot_a], at(*o)) for o in far_first(yc)], ra.at[pl.ds(0, 15)])
+
+    for o in far_first(xz):
+        @pl.when(rank_of(o) < rank)
+        def _():
+            signal(late, at(*o))
 
     loads[3].wait()
     inner, edge = pl.ds(1, Y), 1 + own
@@ -198,6 +218,11 @@
     wait_bytes(rsem.at[0], ra.at[pl.ds(0, 15)])
     slot_b = x * 8 + z
     rb[slot_b] = jnp.sum(ra[...], axis=0)
+
+    @pl.when(rank < 31)
+    def _():
+        pl.semaphore_wait(late, 31 - rank)
+
     start(4, [(0, rb.at[slot_b], rb.at[slot_b], at(*o)) for o in far_first(xz)], rb.at[pl.ds(0, 31)])
 
     wait_bytes(rsem.at[1], rim_bytes)
@@ -362,19 +387,12 @@
         ref = place(base, me, size)
         ref[...] = buf[...].reshape(size, C).astype(BF16)
         for k in ring(n):
-            send(out, ref, ref, at(**{axis: k}), gsem.at[out - 18, k])
+            send(out, ref, ref, at(**{axis: k}))
         pending.append((out, gwbuf.at[pl.ds(0, (n - 1) * size)]))
-    for stage, buf, out, onward, n, me, axis, base, size in spans:
-        ref = place(base, me, size)
-        send(onward, ref, ref, other)
-        pending.append((onward, gwbuf.at[pl.ds(0, n * size)]))
-    for far in range(1, 5):
-        for stage, buf, out, onward, n, me, axis, base, size in spans:
-            for k in range(1, n):
-                if hops(k, n) == far:
-                    ref = place(base, (me - k) % n, size)
-                    wait_bytes(gsem.at[out - 18, k], ref)
-                    send(onward, ref, ref, other)
+    for stage, buf, out, onward, n, me, axis, base, size in spans[2:] + spans[:2]:
+        wait_bytes(rsem.at[out], gwbuf.at[pl.ds(0, (n - 1) * size)])
+        ref = gwbuf.at[pl.ds(pl.multiple_of(half + base, 64), n * size)]
+        start(onward, [(0, ref, ref, other)], gwbuf.at[pl.ds(0, n * size)])
 
     def write_half(core, base):
         moves = [(t * C, core * 18 * C + t * C, C) for t in range(9)]
@@ -447,7 +465,7 @@
             pltpu.SemaphoreType.DMA((9,)),
             pltpu.SemaphoreType.DMA((24,)),
             pltpu.SemaphoreType.DMA((24,)),
-            pltpu.SemaphoreType.DMA((3, 8)),
+            pltpu.SemaphoreType.REGULAR,
         ],
         compiler_params=pltpu.CompilerParams(
             collective_id=0, has_side_effects=True, vmem_limit_bytes=40 * 2**20

time: 56.2 us -> 55.6 us (0.989)
  Pallas kernels: 55.4 us -> 54.7 us
    pallas_call x1, Pallas kernels: 54.4 us -> 53.7 us  [on_device(): pl.pallas_call(functools.partial(kernel, total_voxels), out_shape=shapes,...]
where the time goes in v4:
time: 55.6 us; the launch traced here: 55.4 us
  Pallas kernels  54.7 us (98%)
  between operations  0.64 us (1%)
    pallas_call x1, Pallas kernels, on_device(): pl.pallas_call(functools.partial(kernel, total_voxels), out_shape=shapes,...  53.7 us

profile of v4, /device:TPU:1, one launch (start us, length us, event | category | flops | bytes accessed | tf_op | source)
XLA Modules:
  0.0 55.4 jit_solution(4970688653868938577)
XLA Ops:
  0.6 53.7 %conv_block_backward.1 = (bf16[2,12,32,128]{3,2,1,0:T(8,128)(2,1)S(1)}, bf16[3456,128]{1,0:T(8,128)(2,1)S(1)}, f32[1,128]{1,0:T(1,128)S(1)}, f32[1,128]{1,0:T(1,128)S(1)}) custom-call(bf16[2,12,32,128]{3,2,1,0:T(8,128)(2,1)} %feat.1, bf16[2,12,32,128]{3,2,1,0:T(8,128)(2,1)} %conv.1, bf16[2,12,32,128]{3,2,1,0:T(8,128)(2,1)} %activ.1, ...), custom_call_target="tpu_custom_call" | custom-call | tf_op jit(solution)/shard_map/conv_block_backward/pallas_call | solution.py:438
  54.4 1.0 %copy_outputs.1 = (bf16[2,12,32,128]{3,2,1,0:T(8,128)(2,1)}, bf16[3456,128]{1,0:T(8,128)(2,1)}, f32[1,128]{1,0:T(1,128)}, f32[1,128]{1,0:T(1,128)}) custom-call(bf16[2,12,32,128]{3,2,1,0:T(8,128)(2,1)S(1)} %get-tuple-element.12.refs_0_, bf16[3456,128]{1,0:T(8,128)(2,1)S(1)} %get-tuple-element.13.refs_1_, f32[1,128]{1,0:T(1,128)S(1)} %get-tuple-element.14.refs_2_, ...), custom_call_target="tpu_custom_call" | custom-call | tf_op jit(solution)/shard_map/copy_outputs/pallas_call | solution.py:475

commit v5 on v4

--- a/solution.py
+++ b/solution.py
@@ -188,12 +188,12 @@
     slot_a = c * 8 + y
     ra[slot_a] = stats
     pl.semaphore_wait(barrier, len(partners) + rank)
-    start(0, [(0, ra.at[slot_a], ra.at[slot_a], at(*o)) for o in far_first(yc)], ra.at[pl.ds(0, 15)])
-
     for o in far_first(xz):
         @pl.when(rank_of(o) < rank)
         def _():
             signal(late, at(*o))
+
+    start(0, [(0, ra.at[slot_a], ra.at[slot_a], at(*o)) for o in far_first(yc)], ra.at[pl.ds(0, 15)])
 
     loads[3].wait()
     inner, edge = pl.ds(1, Y), 1 + own
@@ -309,6 +309,11 @@
             acc = acc + buf[j].astype(F32)
         return acc
 
+    wait_bytes(rsem.at[7], x1.at[pl.ds(0, 3)])
+    s2x[...] = add_up(x1, 4).reshape(8, XP // 8, C)
+    x2[y] = s2x[y]
+    start(10, ring_sends(8, y, "dy", lambda j: s2x.at[j], lambda j: x2.at[j]), x2.at[pl.ds(0, 7)])
+
     wait_bytes(rsem.at[5], y1.at[pl.ds(0, 7)])
     s2y[...] = add_up(y1, 8).reshape(8, YP // 8, C)
     y2[z] = s2y[z]
@@ -317,11 +322,6 @@
     s2z[...] = add_up(z1, 8).reshape(8, ZP // 8, C)
     z2[y] = s2z[y]
     start(9, ring_sends(8, y, "dy", lambda j: s2z.at[j], lambda j: z2.at[j]), z2.at[pl.ds(0, 7)])
-    wait_bytes(rsem.at[7], x1.at[pl.ds(0, 3)])
-    s2x[...] = add_up(x1, 4).reshape(8, XP // 8, C)
-    x2[y] = s2x[y]
-    start(10, ring_sends(8, y, "dy", lambda j: s2x.at[j], lambda j: x2.at[j]), x2.at[pl.ds(0, 7)])
-
     inner_x = pl.ds(1, X)
     moves = [
         (X, inner, 0, inner, (up_x, gy)),

time: 55.6 us -> 55 us (0.989)
  no operation moved by 1% of the time
where the time goes in v5:
time: 55 us; the launch traced here: 54.9 us
  Pallas kernels  54.2 us (99%)
  between operations  0.64 us (1%)
    pallas_call x1, Pallas kernels, on_device(): pl.pallas_call(functools.partial(kernel, total_voxels), out_shape=shapes,...  53.2 us

profile of v5, /device:TPU:1, one launch (start us, length us, event | category | flops | bytes accessed | tf_op | source)
XLA Modules:
  0.0 54.9 jit_solution(8329524097170113786)
XLA Ops:
  0.6 53.2 %conv_block_backward.1 = (bf16[2,12,32,128]{3,2,1,0:T(8,128)(2,1)S(1)}, bf16[3456,128]{1,0:T(8,128)(2,1)S(1)}, f32[1,128]{1,0:T(1,128)S(1)}, f32[1,128]{1,0:T(1,128)S(1)}) custom-call(bf16[2,12,32,128]{3,2,1,0:T(8,128)(2,1)} %feat.1, bf16[2,12,32,128]{3,2,1,0:T(8,128)(2,1)} %conv.1, bf16[2,12,32,128]{3,2,1,0:T(8,128)(2,1)} %activ.1, ...), custom_call_target="tpu_custom_call" | custom-call | tf_op jit(solution)/shard_map/conv_block_backward/pallas_call | solution.py:438
  53.8 1.0 %copy_outputs.1 = (bf16[2,12,32,128]{3,2,1,0:T(8,128)(2,1)}, bf16[3456,128]{1,0:T(8,128)(2,1)}, f32[1,128]{1,0:T(1,128)}, f32[1,128]{1,0:T(1,128)}) custom-call(bf16[2,12,32,128]{3,2,1,0:T(8,128)(2,1)S(1)} %get-tuple-element.12.refs_0_, bf16[3456,128]{1,0:T(8,128)(2,1)S(1)} %get-tuple-element.13.refs_1_, f32[1,128]{1,0:T(1,128)S(1)} %get-tuple-element.14.refs_2_, ...), custom_call_target="tpu_custom_call" | custom-call | tf_op jit(solution)/shard_map/copy_outputs/pallas_call | solution.py:475
